TPU v7x, 32 devices: a whole 2x2x4 slice. The times are simulated.
32 devices in a mesh: fsdp: 4 (over z), ctx: 8 (over y, x, core).
Axes of the slice: x: 2, y: 2, z: 4, core: 2. Of those that a mesh axis runs over, the one named last changes fastest.
Arguments:
- hidden_in: bfloat16 [8, 2048, 1024], P('fsdp', 'ctx'), may hold values from -6 to 6
- cotangent: bfloat16 [8, 2048, 1024], P('fsdp', 'ctx'), may hold values from -6 to 6
- segments: int32 [8, 2048], P('fsdp'), may hold values from 0 to 3, as said below
- entry_gain: bfloat16 [1024], P('fsdp'), may hold values from 0.5 to 1.5
- query_weight: bfloat16 [1024, 512], P('fsdp'), may hold values from -0.1875 to 0.1875
- key_weight: bfloat16 [1024, 128], P('fsdp'), may hold values from -0.1875 to 0.1875
- value_weight: bfloat16 [1024, 128], P('fsdp'), may hold values from -0.1875 to 0.1875
- output_weight: bfloat16 [512, 1024], P('fsdp'), may hold values from -1.5 to 1.5
- mixer_weight: bfloat16 [1024, 3328], P('fsdp'), may hold values from -0.1875 to 0.1875
- step_weight: bfloat16 [1024, 24], P('fsdp'), may hold values from -0.1875 to 0.1875
- conv_weight: bfloat16 [4, 1792], P(None, 'fsdp'), may hold values from -3 to 3
- conv_bias: bfloat16 [1792], P('fsdp'), may hold values from -3 to 3
- step_offset: bfloat16 [24], P('fsdp'), may hold values from -1 to 1
- decay_rate: bfloat16 [24], P('fsdp'), may hold values from 0 to 1, as said below
- skip_weight: bfloat16 [24], P('fsdp'), may hold values from -1 to 1
- gated_gain: bfloat16 [1536], P('fsdp'), may hold values from 0.5 to 1.5
- merge_weight: bfloat16 [1536, 1024], P('fsdp'), may hold values from -0.15625 to 0.15625
- second_gain: bfloat16 [1024], P('fsdp'), may hold values from 0.5 to 1.5
- gate_weight: bfloat16 [1024, 2048], P('fsdp'), may hold values from -0.1875 to 0.1875
- up_weight: bfloat16 [1024, 2048], P('fsdp'), may hold values from -0.1875 to 0.1875
- down_weight: bfloat16 [2048, 1024], P('fsdp'), may hold values from -0.125 to 0.125
Outputs:
- block_out: float32 [8, 2048, 1024], P('fsdp', 'ctx')
- tokens_grad: float32 [8, 2048, 1024], P('fsdp', 'ctx')
- entry_grad: float32 [1024], P('fsdp')
- query_grad: float32 [1024, 512], P('fsdp')
- key_grad: float32 [1024, 128], P('fsdp')
- value_grad: float32 [1024, 128], P('fsdp')
- output_grad: float32 [512, 1024], P('fsdp')
- mixer_grad: float32 [1024, 3328], P('fsdp')
- step_grad: float32 [1024, 24], P('fsdp')
- conv_grad: float32 [4, 1792], P(None, 'fsdp')
- bias_grad: float32 [1792], P('fsdp')
- offset_grad: float32 [24], P('fsdp')
- decay_grad: float32 [24], P('fsdp')
- skip_grad: float32 [24], P('fsdp')
- gated_grad: float32 [1536], P('fsdp')
- merge_grad: float32 [1536, 1024], P('fsdp')
- second_grad: float32 [1024], P('fsdp')
- gate_grad: float32 [1024, 2048], P('fsdp')
- up_grad: float32 [1024, 2048], P('fsdp')
- down_grad: float32 [2048, 1024], P('fsdp')
Inputs may be any that keep to these rules, and one draw needn't show every extreme that they name: `segments`: within each sequence the numbers start at 0, never fall and rise by at most one from a token to the next; every document has 204 tokens or more; of each 2 consecutive sequences one is a single document, and every other sequence holds four documents. `decay_rate`: per-head rates between 0.1 / 2048 and 64 / 2048.
All inputs are finite; a program needn't handle non-finite values.
Results may differ from a plain program's by a relative error of at most 0.019.
The roundings to bfloat16 on the way count: a program that leaves them out, or rounds other values in their place, can miss the bound.
Values may be sent and summed in bfloat16 or wider, within the bound.
A program may use at most 384 MiB of HBM per device.

v0:
```python
import jax
import jax.numpy as jnp
from jax import lax
from jax.sharding import PartitionSpec as P

QHEADS = 8
KVHEADS = 2
HEAD = 64
MHEADS = 24
MHEAD = 64
STATE = 128
CONVW = 4
QW = 512
KW = 128
DS = 1536
PROJ = 3328


EPSILON = 1e-05
ROPE_BASE = 10000.0
SCORE_SCALE = 0.125
PRECISE = lax.Precision.HIGHEST


def shifted(block, axis, distance):
    devices = range(lax.axis_size(axis))
    route = [(i - distance, i) for i in devices if i - distance in devices]
    return lax.ppermute(block, axis, route)


def prefix_2(value, axis, join, neutral, backward):
    count, mine = (lax.axis_size(axis), lax.axis_index(axis))
    pieces = jax.tree.map(lambda part: lax.all_gather(part, axis), value)
    if backward:
        pieces = jax.tree.map(lambda part: part[::-1], pieces)
        mine = count - 1 - mine
    running = jax.tree.map(
        lambda part, zero: jnp.full_like(part, 0) + jnp.asarray(zero, part.dtype), value, neutral
    )

    def lap(position, running):
        longer = join(running, jax.tree.map(lambda part: part[position], pieces))
        return jax.tree.map(lambda new, old: jnp.where(position < mine, new, old), longer, running)

    return lax.fori_loop(0, count - 1, lap, running)


def matmul(left, right):
    return jnp.dot(left, right, preferred_element_type=jnp.float32)


def weight_grad(left, right):
    return jnp.einsum("rd,rf->df", left, right, preferred_element_type=jnp.float32)


def back_product(grads_in, weight):
    return jnp.einsum("rf,df->rd", grads_in, weight, preferred_element_type=jnp.float32)


def root_norm(values, gain):
    return values * lax.rsqrt(jnp.mean(values * values, axis=-1, keepdims=True) + EPSILON) * gain


def rotate(heads, places):
    half_dim = heads.shape[-1] // 2
    freqs = ROPE_BASE ** (-2.0 * jnp.arange(half_dim, dtype=jnp.float32) / heads.shape[-1])
    angles = places.astype(jnp.float32)[:, None] * freqs[None, :]
    cosine = jnp.cos(angles)[:, None, :]
    sine = jnp.sin(angles)[:, None, :]
    front = heads[..., :half_dim]
    behind = heads[..., half_dim:]
    return jnp.concatenate(
        [front * cosine - behind * sine, behind * cosine + front * sine], axis=-1
    )


def block_decays(log_decay, segment):
    cumulate = jnp.cumsum(log_decay, axis=0)
    ordinal = jnp.arange(segment.shape[0], dtype=jnp.int32)
    related = (segment[:, None] == segment[None, :]) & (ordinal[:, None] >= ordinal[None, :])
    log_gap = jnp.where(related[:, :, None], cumulate[:, None, :] - cumulate[None, :, :], 0.0)
    return (cumulate, jnp.where(related[:, :, None], jnp.exp(log_gap), 0.0))


def block_state(ssm_input, in_matrix, step_size, log_decay, segment, prior_segment):
    cumulate = jnp.cumsum(log_decay, axis=0)
    tail_decay = (
        jnp.where((segment == segment[-1])[:, None], jnp.exp(cumulate[-1][None, :] - cumulate), 0.0)
        * step_size
    )
    local_state = jnp.einsum("jh,jhp,jn->hpn", tail_decay, ssm_input, in_matrix, precision=PRECISE)
    through = jnp.where(segment[-1] == prior_segment, jnp.exp(cumulate[-1]), 0.0)
    return (through, local_state)


def block_output(
    ssm_state, ssm_input, in_matrix, out_matrix, step_size, log_decay, segment, prior_segment
):
    cumulate, decays = block_decays(log_decay, segment)
    intersection = jnp.dot(out_matrix, in_matrix.T, precision=PRECISE)
    mixing = decays * intersection[:, :, None] * step_size[None, :, :]
    result = jnp.einsum("ijh,jhp->ihp", mixing, ssm_input, precision=PRECISE)
    carry_in = jnp.where((segment == prior_segment)[:, None], jnp.exp(cumulate), 0.0)
    return result + carry_in[:, :, None] * jnp.einsum(
        "in,hpn->ihp", out_matrix, ssm_state, precision=PRECISE
    )


def mamba_front(
    projected,
    rim_rows,
    step_raw,
    segment_ext,
    prior_segment,
    conv_taps,
    conv_shift,
    step_shift,
    decay_speed,
):
    length = projected.shape[0]
    back_reach = CONVW - 1
    conv_input = jnp.concatenate([rim_rows, projected[:, DS:]], axis=0)
    segment = segment_ext[back_reach:]
    summed = conv_input[back_reach:] * conv_taps[back_reach]
    for offset in range(1, CONVW):
        start_row = back_reach - offset
        earlier = conv_input[start_row : start_row + length]
        related = segment_ext[start_row : start_row + length] == segment
        summed = summed + jnp.where(related[:, None], earlier, 0.0) * conv_taps[start_row]
    activated = jax.nn.silu(summed + conv_shift)
    ssm_input = activated[:, :DS].reshape(length, MHEADS, MHEAD)
    in_matrix = activated[:, DS : DS + STATE]
    out_matrix = activated[:, DS + STATE :]
    step_size = jax.nn.softplus(step_raw + step_shift)
    log_decay = -step_size * decay_speed
    chain = block_state(ssm_input, in_matrix, step_size, log_decay, segment, prior_segment)
    return ((ssm_input, in_matrix, out_matrix, step_size, log_decay), chain)


def mamba_tail(ssm_state, inside, mixer_gate, segment, prior_segment, skip_scale, gated_scale):
    ssm_input, in_matrix, out_matrix, step_size, log_decay = inside
    length = mixer_gate.shape[0]
    ssm_out = (
        block_output(
            ssm_state,
            ssm_input,
            in_matrix,
            out_matrix,
            step_size,
            log_decay,
            segment,
            prior_segment,
        )
        + skip_scale[None, :, None] * ssm_input
    )
    gated_out = ssm_out.reshape(length, DS) * jax.nn.silu(mixer_gate)
    return root_norm(gated_out, gated_scale)


def chain_combine(earlier, later):
    return (earlier[0] * later[0], later[0][..., None, None] * earlier[1] + later[1])


def score_weights(query_block, key_block, segment_here, segment_full, places):
    length = query_block.shape[0]
    seq_span = key_block.shape[0]
    group_size = QHEADS // KVHEADS
    query_heads = query_block.reshape(length, KVHEADS, group_size, HEAD)
    key_heads = key_block.reshape(seq_span, KVHEADS, HEAD)
    raw_scores = (
        jnp.einsum("qgrd,kgd->grqk", query_heads, key_heads, preferred_element_type=jnp.float32)
        * SCORE_SCALE
    )
    allowed = (segment_here[:, None] == segment_full[None, :]) & (
        places[:, None] >= jnp.arange(seq_span, dtype=jnp.int32)[None, :]
    )
    masked = jnp.where(allowed[None, None], raw_scores, -1e30)
    highest = jnp.max(masked, axis=-1, keepdims=True)
    weights = jnp.exp(masked - highest)
    return weights / jnp.sum(weights, axis=-1, keepdims=True)


def attend_forward(pieces, places):
    query_block, key_block, value_block, segment_here, segment_full = pieces
    length = query_block.shape[0]
    probability = score_weights(query_block, key_block, segment_here, segment_full, places)
    value_heads = value_block.reshape(key_block.shape[0], KVHEADS, HEAD)
    mixed = jnp.einsum(
        "grqk,kgd->qgrd",
        probability.astype(jnp.bfloat16),
        value_heads,
        preferred_element_type=jnp.float32,
    )
    return mixed.reshape(length, QHEADS * HEAD)


def attend_backward(pieces, places):
    query_block, key_block, value_block, segment_here, segment_full, delta_block = pieces
    length = query_block.shape[0]
    seq_span = key_block.shape[0]
    group_size = QHEADS // KVHEADS
    probability = score_weights(query_block, key_block, segment_here, segment_full, places)
    key_heads = key_block.reshape(seq_span, KVHEADS, HEAD)
    value_heads = value_block.reshape(seq_span, KVHEADS, HEAD)
    delta_heads = delta_block.reshape(length, KVHEADS, group_size, HEAD)
    weight_delta = jnp.einsum(
        "qgrd,kgd->grqk", delta_heads, value_heads, preferred_element_type=jnp.float32
    )
    centre = jnp.sum(weight_delta * probability, axis=-1, keepdims=True)
    score_low = (probability * (weight_delta - centre)).astype(jnp.bfloat16)
    query_delta = (
        jnp.einsum("grqk,kgd->qgrd", score_low, key_heads, preferred_element_type=jnp.float32)
        * SCORE_SCALE
    )
    return (query_delta.reshape(length, QHEADS * HEAD), score_low, probability.astype(jnp.bfloat16))


def per_device(
    hidden_in,
    cotangent,
    segments,
    entry_gain,
    query_weight,
    key_weight,
    value_weight,
    output_weight,
    mixer_weight,
    step_weight,
    conv_weight,
    conv_bias,
    step_offset,
    decay_rate,
    skip_weight,
    gated_gain,
    merge_weight,
    second_gain,
    gate_weight,
    up_weight,
    down_weight,
):
    gathered = (
        lax.all_gather(entry_gain, "fsdp", axis=0, tiled=True),
        lax.all_gather(query_weight, "fsdp", axis=0, tiled=True),
        lax.all_gather(key_weight, "fsdp", axis=0, tiled=True),
        lax.all_gather(value_weight, "fsdp", axis=0, tiled=True),
        lax.all_gather(output_weight, "fsdp", axis=0, tiled=True),
        lax.all_gather(mixer_weight, "fsdp", axis=0, tiled=True),
        lax.all_gather(step_weight, "fsdp", axis=0, tiled=True),
        lax.all_gather(conv_weight, "fsdp", axis=1, tiled=True),
        lax.all_gather(conv_bias, "fsdp", axis=0, tiled=True),
        lax.all_gather(step_offset, "fsdp", axis=0, tiled=True),
        lax.all_gather(decay_rate, "fsdp", axis=0, tiled=True),
        lax.all_gather(skip_weight, "fsdp", axis=0, tiled=True),
        lax.all_gather(gated_gain, "fsdp", axis=0, tiled=True),
        lax.all_gather(merge_weight, "fsdp", axis=0, tiled=True),
        lax.all_gather(second_gain, "fsdp", axis=0, tiled=True),
        lax.all_gather(gate_weight, "fsdp", axis=0, tiled=True),
        lax.all_gather(up_weight, "fsdp", axis=0, tiled=True),
        lax.all_gather(down_weight, "fsdp", axis=0, tiled=True),
    )
    (
        entry_full,
        query_full,
        key_full,
        value_full,
        output_full,
        mixer_full,
        step_full,
        conv_full,
        bias_full,
        offset_full,
        decay_full,
        skip_full,
        gated_full,
        merge_full,
        second_full,
        gate_full,
        up_full,
        down_full,
    ) = gathered
    entry_scale = entry_full.astype(jnp.float32)
    conv_taps = conv_full.astype(jnp.float32)
    conv_shift = bias_full.astype(jnp.float32)
    step_shift = offset_full.astype(jnp.float32)
    decay_speed = decay_full.astype(jnp.float32)
    skip_scale = skip_full.astype(jnp.float32)
    gated_scale = gated_full.astype(jnp.float32)
    second_scale = second_full.astype(jnp.float32)
    batches, length, features = hidden_in.shape
    flat_rows = batches * length
    back_reach = CONVW - 1
    group_size = QHEADS // KVHEADS
    anchor = lax.axis_index("ctx") * length
    places = anchor + jnp.arange(length, dtype=jnp.int32)
    padded_segments = jnp.concatenate(
        [jnp.full((batches, back_reach), -1, jnp.int32), segments], axis=1
    )
    segment_ext = lax.dynamic_slice_in_dim(padded_segments, anchor, length + back_reach, 1)
    segment_here = segment_ext[:, back_reach:]
    prior_segment = segment_ext[:, back_reach - 1]
    tokens = hidden_in.reshape(flat_rows, features).astype(jnp.float32)
    normed = root_norm(tokens, entry_scale).astype(jnp.bfloat16)
    queries = (
        rotate(matmul(normed, query_full).reshape(batches, length, QHEADS, HEAD), places)
        .astype(jnp.bfloat16)
        .reshape(batches, length, QW)
    )
    key_rows = (
        rotate(matmul(normed, key_full).reshape(batches, length, KVHEADS, HEAD), places)
        .astype(jnp.bfloat16)
        .reshape(batches, length, KW)
    )
    value_rows = matmul(normed, value_full).astype(jnp.bfloat16).reshape(batches, length, KW)
    all_keys, all_values = (
        lax.all_gather(key_rows, "ctx", axis=1, tiled=True),
        lax.all_gather(value_rows, "ctx", axis=1, tiled=True),
    )
    attended = lax.map(
        lambda pieces: attend_forward(pieces, places),
        (queries, all_keys, all_values, segment_here, segments),
    )
    attended_low = attended.reshape(flat_rows, QW).astype(jnp.bfloat16)
    projected = matmul(normed, mixer_full).reshape(batches, length, PROJ)
    step_raw = matmul(normed, step_full).reshape(batches, length, MHEADS)
    rim_rows = shifted(projected[:, length - back_reach :, DS:], "ctx", 1)
    front_map = jax.vmap(mamba_front, in_axes=(0, 0, 0, 0, 0, None, None, None, None))
    tail_map = jax.vmap(mamba_tail, in_axes=(0, 0, 0, 0, 0, None, None))
    inside, chain = front_map(
        projected,
        rim_rows,
        step_raw,
        segment_ext,
        prior_segment,
        conv_taps,
        conv_shift,
        step_shift,
        decay_speed,
    )
    through_decay, local_state = chain
    prefix = prefix_2(
        (through_decay, local_state),
        "ctx",
        chain_combine,
        (jnp.ones_like(through_decay), jnp.zeros_like(local_state)),
        False,
    )
    state_in = prefix[1]
    mixer_gate = projected[:, :, :DS]
    mixed = tail_map(
        state_in, inside, mixer_gate, segment_here, prior_segment, skip_scale, gated_scale
    )
    mixed_low = mixed.reshape(flat_rows, DS).astype(jnp.bfloat16)
    middle = tokens + matmul(attended_low, output_full) + matmul(mixed_low, merge_full)
    second = root_norm(middle, second_scale).astype(jnp.bfloat16)
    gate_proj = matmul(second, gate_full)
    up_proj = matmul(second, up_full)
    hidden = (jax.nn.silu(gate_proj) * up_proj).astype(jnp.bfloat16)
    block_out = (middle + matmul(hidden, down_full)).reshape(batches, length, features)
    regathered = (
        lax.all_gather(query_weight, "fsdp", axis=0, tiled=True),
        lax.all_gather(key_weight, "fsdp", axis=0, tiled=True),
        lax.all_gather(value_weight, "fsdp", axis=0, tiled=True),
        lax.all_gather(output_weight, "fsdp", axis=0, tiled=True),
        lax.all_gather(mixer_weight, "fsdp", axis=0, tiled=True),
        lax.all_gather(step_weight, "fsdp", axis=0, tiled=True),
        lax.all_gather(merge_weight, "fsdp", axis=0, tiled=True),
        lax.all_gather(gate_weight, "fsdp", axis=0, tiled=True),
        lax.all_gather(up_weight, "fsdp", axis=0, tiled=True),
        lax.all_gather(down_weight, "fsdp", axis=0, tiled=True),
    )
    (
        query_back,
        key_back,
        value_back,
        output_back,
        mixer_back,
        step_back,
        merge_back,
        gate_back,
        up_back,
        down_back,
    ) = regathered
    incoming = cotangent.reshape(flat_rows, features)
    down_grad = weight_grad(hidden, incoming)
    hidden_delta = back_product(incoming, down_back)
    _, swiglu_pull = jax.vjp(
        lambda gate_in, up_in: jax.nn.silu(gate_in) * up_in, gate_proj, up_proj
    )
    gate_delta, up_delta = swiglu_pull(hidden_delta)
    gate_low = gate_delta.astype(jnp.bfloat16)
    up_low = up_delta.astype(jnp.bfloat16)
    gate_grad = weight_grad(second, gate_low)
    up_grad = weight_grad(second, up_low)
    second_delta = back_product(gate_low, gate_back) + back_product(up_low, up_back)
    _, second_pull = jax.vjp(root_norm, middle, second_scale)
    middle_norm_delta, second_grad = second_pull(second_delta)
    middle_delta = incoming.astype(jnp.float32) + middle_norm_delta
    branch_low = middle_delta.astype(jnp.bfloat16)
    output_grad = weight_grad(attended_low, branch_low)
    merge_grad = weight_grad(mixed_low, branch_low)
    attended_delta = (
        back_product(branch_low, output_back).astype(jnp.bfloat16).reshape(batches, length, QW)
    )
    mixed_delta = (
        lax.optimization_barrier(back_product(branch_low, merge_back).astype(jnp.bfloat16))
        .astype(jnp.float32)
        .reshape(batches, length, DS)
    )

    def tail_apply(state_value, inside_value, gate_value, skip_value, gain_value):
        return tail_map(
            state_value,
            inside_value,
            gate_value,
            segment_here,
            prior_segment,
            skip_value,
            gain_value,
        )

    _, tail_pull = jax.vjp(tail_apply, state_in, inside, mixer_gate, skip_scale, gated_scale)
    state_delta, inside_delta, gate_z_delta, skip_grad, gated_grad = tail_pull(mixed_delta)
    suffix = prefix_2(
        (through_decay, state_delta),
        "ctx",
        chain_combine,
        (jnp.ones_like(through_decay), jnp.zeros_like(state_delta)),
        True,
    )
    carried_delta = suffix[1]
    through_delta = jnp.sum(carried_delta * state_in, axis=(2, 3))

    def front_apply(
        proj_value, rim_value, step_value, taps_value, shift_value, offset_value, decay_value
    ):
        return front_map(
            proj_value,
            rim_value,
            step_value,
            segment_ext,
            prior_segment,
            taps_value,
            shift_value,
            offset_value,
            decay_value,
        )

    _, front_pull = jax.vjp(
        front_apply, projected, rim_rows, step_raw, conv_taps, conv_shift, step_shift, decay_speed
    )
    proj_delta, rim_delta, step_delta, conv_grad, bias_grad, offset_grad, decay_grad = front_pull(
        (inside_delta, (through_delta, carried_delta))
    )
    rim_back = shifted(rim_delta, "ctx", -1)
    proj_total = jnp.concatenate([gate_z_delta, proj_delta[:, :, DS:]], axis=2)
    proj_total = proj_total.at[:, length - back_reach :, DS:].add(rim_back)
    proj_low = proj_total.reshape(flat_rows, PROJ).astype(jnp.bfloat16)
    step_low = step_delta.reshape(flat_rows, MHEADS).astype(jnp.bfloat16)
    mixer_grad = weight_grad(normed, proj_low)
    step_grad = weight_grad(normed, step_low)
    normed_delta = back_product(proj_low, mixer_back) + back_product(step_low, step_back)
    back_keys, back_values = (all_keys, all_values)
    query_delta, score_low, weight_low = lax.map(
        lambda pieces: attend_backward(pieces, places),
        (queries, back_keys, back_values, segment_here, segments, attended_delta),
    )
    query_heads = queries.reshape(batches, length, KVHEADS, group_size, HEAD)
    delta_heads = attended_delta.reshape(batches, length, KVHEADS, group_size, HEAD)
    row_count = length * lax.axis_size("ctx")
    key_part = (
        jnp.einsum("bgrqk,bqgrd->kbgd", score_low, query_heads, preferred_element_type=jnp.float32)
        * SCORE_SCALE
    )
    value_part = jnp.einsum(
        "bgrqk,bqgrd->kbgd", weight_low, delta_heads, preferred_element_type=jnp.float32
    )
    pair_delta = jnp.swapaxes(
        lax.psum_scatter(
            jnp.concatenate(
                [
                    key_part.reshape(row_count, batches, KW),
                    value_part.reshape(row_count, batches, KW),
                ],
                axis=2,
            ),
            "ctx",
            scatter_dimension=0,
            tiled=True,
        ),
        0,
        1,
    )
    key_low = (
        rotate(pair_delta[:, :, :KW].reshape(batches, length, KVHEADS, HEAD), -places)
        .astype(jnp.bfloat16)
        .reshape(flat_rows, KW)
    )
    value_low = pair_delta[:, :, KW:].astype(jnp.bfloat16).reshape(flat_rows, KW)
    query_low = (
        rotate(query_delta.reshape(batches, length, QHEADS, HEAD), -places)
        .astype(jnp.bfloat16)
        .reshape(flat_rows, QW)
    )
    query_grad = weight_grad(normed, query_low)
    key_grad = weight_grad(normed, key_low)
    value_grad = weight_grad(normed, value_low)
    normed_delta = (
        normed_delta
        + back_product(query_low, query_back)
        + back_product(key_low, key_back)
        + back_product(value_low, value_back)
    )
    _, entry_pull = jax.vjp(root_norm, tokens, entry_scale)
    token_delta, entry_grad = entry_pull(normed_delta)
    tokens_grad = (middle_delta + token_delta).reshape(batches, length, features)
    reduced = (
        lax.psum_scatter(entry_grad, "fsdp", scatter_dimension=0, tiled=True),
        lax.psum_scatter(query_grad, "fsdp", scatter_dimension=0, tiled=True),
        lax.psum_scatter(key_grad, "fsdp", scatter_dimension=0, tiled=True),
        lax.psum_scatter(value_grad, "fsdp", scatter_dimension=0, tiled=True),
        lax.psum_scatter(output_grad, "fsdp", scatter_dimension=0, tiled=True),
        lax.psum_scatter(mixer_grad, "fsdp", scatter_dimension=0, tiled=True),
        lax.psum_scatter(step_grad, "fsdp", scatter_dimension=0, tiled=True),
        lax.psum_scatter(conv_grad, "fsdp", scatter_dimension=1, tiled=True),
        lax.psum_scatter(bias_grad, "fsdp", scatter_dimension=0, tiled=True),
        lax.psum_scatter(offset_grad, "fsdp", scatter_dimension=0, tiled=True),
        lax.psum_scatter(decay_grad, "fsdp", scatter_dimension=0, tiled=True),
        lax.psum_scatter(skip_grad, "fsdp", scatter_dimension=0, tiled=True),
        lax.psum_scatter(gated_grad, "fsdp", scatter_dimension=0, tiled=True),
        lax.psum_scatter(merge_grad, "fsdp", scatter_dimension=0, tiled=True),
        lax.psum_scatter(second_grad, "fsdp", scatter_dimension=0, tiled=True),
        lax.psum_scatter(gate_grad, "fsdp", scatter_dimension=0, tiled=True),
        lax.psum_scatter(up_grad, "fsdp", scatter_dimension=0, tiled=True),
        lax.psum_scatter(down_grad, "fsdp", scatter_dimension=0, tiled=True),
    )
    (
        entry_part,
        query_part,
        key_part,
        value_part,
        output_part,
        mixer_part,
        step_part,
        conv_part,
        bias_part,
        offset_part,
        decay_part,
        skip_part,
        gated_part,
        merge_part,
        second_part,
        gate_part,
        up_part,
        down_part,
    ) = reduced
    totals = lax.psum(
        (
            entry_part,
            query_part,
            key_part,
            value_part,
            output_part,
            mixer_part,
            step_part,
            conv_part,
            bias_part,
            offset_part,
            decay_part,
            skip_part,
            gated_part,
            merge_part,
            second_part,
            gate_part,
            up_part,
            down_part,
        ),
        "ctx",
    )
    (
        entry_sum,
        query_sum,
        key_sum,
        value_sum,
        output_sum,
        mixer_sum,
        step_sum,
        conv_sum,
        bias_sum,
        offset_sum,
        decay_sum,
        skip_sum,
        gated_sum,
        merge_sum,
        second_sum,
        gate_sum,
        up_sum,
        down_sum,
    ) = totals
    return (
        block_out,
        tokens_grad,
        entry_sum,
        query_sum,
        key_sum,
        value_sum,
        output_sum,
        mixer_sum,
        step_sum,
        conv_sum,
        bias_sum,
        offset_sum,
        decay_sum,
        skip_sum,
        gated_sum,
        merge_sum,
        second_sum,
        gate_sum,
        up_sum,
        down_sum,
    )


def solution(mesh):
    placed = (
        P("fsdp", "ctx", None),
        P("fsdp", "ctx", None),
        P("fsdp", None),
        P("fsdp"),
        P("fsdp", None),
        P("fsdp", None),
        P("fsdp", None),
        P("fsdp", None),
        P("fsdp", None),
        P("fsdp", None),
        P(None, "fsdp"),
        P("fsdp"),
        P("fsdp"),
        P("fsdp"),
        P("fsdp"),
        P("fsdp"),
        P("fsdp", None),
        P("fsdp"),
        P("fsdp", None),
        P("fsdp", None),
        P("fsdp", None),
    )
    return jax.shard_map(
        per_device,
        mesh=mesh,
        in_specs=placed,
        out_specs=(
            P("fsdp", "ctx", None),
            P("fsdp", "ctx", None),
            P("fsdp"),
            P("fsdp", None),
            P("fsdp", None),
            P("fsdp", None),
            P("fsdp", None),
            P("fsdp", None),
            P("fsdp", None),
            P(None, "fsdp"),
            P("fsdp"),
            P("fsdp"),
            P("fsdp"),
            P("fsdp"),
            P("fsdp"),
            P("fsdp", None),
            P("fsdp"),
            P("fsdp", None),
            P("fsdp", None),
            P("fsdp", None),
        ),
        check_vma=False,
    )
```

profile of v0, /device:TPU:0, one launch (start us, length us, event | category | flops | bytes accessed | tf_op | source)
XLA Modules:
  0.0 2089.6 jit_solution(9879138480887701067)
XLA Ops:
  9.4 12.6 all-gather.2
  22.0 19.1 all_gather.91
  44.3 19.5 all_gather.89
  68.3 9.0 all-reduce.28
  77.4 13.6 all-gather.3
  91.2 19.4 all_gather.98
  114.5 30.5 %all-gather.26.cloned.1.call-done = bf16[1024,3328]{1,0:T(8,128)(2,1)} async-done(((bf16[256,3328]{1,0:T(8,128)(2,1)}), bf16[1024,3328]{1,0:T(8,128)(2,1)}) %all-gather.26.cloned.1.call-update) | async-done | bytes 6815760 | tf_op jit(solution)/shard_map/all_gather | solution.py:247
  184.9 11.8 all-gather.4
  197.7 12.2 all_gather.101
  215.0 9.6 all-gather.18.cloned.1.call-done
  224.6 45.9 %while.55 = (s32[]{:T(128)}, bf16[2,256,512]{2,1,0:T(8,128)(2,1)}, bf16[2,2048,128]{1,2,0:T(8,128)(2,1)}, s32[2,256]{1,0:T(2,128)S(1)}, s32[2,2048]{1,0:T(2,128)...) while((s32[]{:T(128)}, bf16[2,256,512]{2,1,0:T(8,128)(2,1)}, ...), condition=%wide.region_4.5_spmd.clone, body=%wide.region_1.4_spmd.clone.sunk | while | flops 1100482816 | bytes 39892092 | solution.py:318
  228.0 10.9 fusion.301
  250.5 10.3 fusion.301
  260.8 8.8 fusion.302
  272.4 26.8 %all-gather.36.cloned.1.call-done = f32[16,24,64,128]{3,2,1,0:T(8,128)} async-done(((f32[2,24,64,128]{3,2,1,0:T(8,128)}), f32[16,24,64,128]{3,2,1,0:T(8,128)}) %all-gather.36.cloned.1.call-update) | async-done | bytes 12582928 | tf_op jit(solution)/shard_map/all_gather | solution.py:33
  299.1 12.8 while.57
  316.1 16.3 fusion.73
  340.9 23.2 %all-gather.28.cloned.1.call-done = bf16[1536,1024]{1,0:T(8,128)(2,1)} async-done(((bf16[384,1024]{1,0:T(8,128)(2,1)}), bf16[1536,1024]{1,0:T(8,128)(2,1)}) %all-gather.28.cloned.1.call-update) | async-done | bytes 3145744 | tf_op jit(solution)/shard_map/all_gather | solution.py:255
  369.2 23.1 %all-gather.24.cloned.1.call-done = bf16[512,1024]{1,0:T(8,128)(2,1)} async-done(((bf16[128,1024]{1,0:T(8,128)(2,1)}), bf16[512,1024]{1,0:T(8,128)(2,1)}) %all-gather.24.cloned.1.call-update) | async-done | bytes 1048592 | tf_op jit(solution)/shard_map/all_gather | solution.py:246
  395.5 78.6 %all-gather.32.cloned.1.call-done = bf16[1024,2048]{1,0:T(8,128)(2,1)} async-done(((bf16[256,2048]{1,0:T(8,128)(2,1)}), bf16[1024,2048]{1,0:T(8,128)(2,1)}) %all-gather.32.cloned.1.call-update) | async-done | bytes 4194320 | tf_op jit(solution)/shard_map/all_gather | solution.py:258
  480.6 74.4 %all-gather.30.cloned.1.call-done = bf16[1024,2048]{1,0:T(8,128)(2,1)} async-done(((bf16[256,2048]{1,0:T(8,128)(2,1)}), bf16[1024,2048]{1,0:T(8,128)(2,1)}) %all-gather.30.cloned.1.call-update) | async-done | bytes 4194320 | tf_op jit(solution)/shard_map/all_gather | solution.py:257
  561.9 73.8 %all-gather.34.cloned.1.call-done = bf16[2048,1024]{1,0:T(8,128)(2,1)} async-done(((bf16[512,1024]{1,0:T(8,128)(2,1)}), bf16[2048,1024]{1,0:T(8,128)(2,1)}) %all-gather.34.cloned.1.call-update) | async-done | bytes 4194320 | tf_op jit(solution)/shard_map/all_gather | solution.py:259
  635.8 8.9 multiply_convert_fusion
  658.5 97.9 %while.56 = (s32[]{:T(128)}, f32[2,256,512]{1,2,0:T(8,128)}, bf16[2,2,4,256,2048]{3,4,2,1,0:T(8,128)(2,1)}, bf16[2,2,4,256,2048]{3,4,2,1,0:T(8,128)(2,1)}, bf16[...) while((s32[]{:T(128)}, f32[2,256,512]{1,2,0:T(8,128)}, ...), condition=%wide.region_30.31_spmd.clone, body=%wide.region_26.30_spmd.clone.sunk | while | flops 1662648576 | bytes 134288592 | solution.py:463
  662.7 10.3 fusion.310
  673.1 14.1 fusion.311
  687.2 17.8 bitcast_dynamic-update-slice_fusion.3
  711.6 10.3 fusion.310
  721.9 14.2 fusion.311
  736.1 17.7 bitcast_dynamic-update-slice_fusion.3
  756.4 11.3 fusion.110
  769.9 10.9 fusion.83
  816.2 20.9 reduce-scatter.15.cloned.1.call-done
  878.8 22.5 %fusion.41 = (f32[2,256,24]{1,2,0:T(8,128)}, f32[2,256,24]{1,2,0:T(8,128)}, f32[2,256,24]{1,2,0:T(8,128)}, f32[2,256,256]{2,1,0:T(8,128)S(1)}) fusion(f32[2,256,24]{1,2,0:T(8,128)S(1)} %copy-done.110, f32[2,256,256]{2,1,0:T(8,128)S(1)} %copy-done.69, f32[2,256,24]{1,2,0:T(8,128)S(1)} %copy-done.85, pred[2,256,256]{2,1,0:T(8,128)(4,1)} %copy-done.86, ...), kind=kOutput, calls=%fused_computation.74 | convolution fusion | flops 2462937088 | bytes 7716864 | tf_op jit(solution)/shard_map/transpose(jvp(vmap(ijh,jhp->ihp)))/dot_general | solution.py:102
  911.7 11.9 rev.7
  923.6 12.7 while.58
  941.4 12.7 fusion.72
  985.4 10.9 convolution_bitcast_fusion
  1027.7 22.2 %reduce-scatter.21.cloned.1.call-done = f32[256,128]{1,0:T(8,128)} async-done(((f32[1024,128]{1,0:T(8,128)}), f32[256,128]{1,0:T(8,128)}) %reduce-scatter.21.cloned.1.call-update) | async-done | bytes 131088 | tf_op jit(solution)/shard_map/reduce_scatter | solution.py:520
  1049.9 111.3 %reduce-scatter.29.cloned.1.call-done = f32[384,1024]{1,0:T(8,128)} async-done(((f32[1536,1024]{1,0:T(8,128)}), f32[384,1024]{1,0:T(8,128)}) %reduce-scatter.29.cloned.1.call-update) | async-done | bytes 1572880 | tf_op jit(solution)/shard_map/reduce_scatter | solution.py:530
  1161.2 147.4 %reduce-scatter.33.cloned.1.call-done = f32[256,2048]{1,0:T(8,128)} async-done(((f32[1024,2048]{1,0:T(8,128)}), f32[256,2048]{1,0:T(8,128)}) %reduce-scatter.33.cloned.1.call-update) | async-done | bytes 2097168 | tf_op jit(solution)/shard_map/reduce_scatter | solution.py:533
  1308.5 147.7 %reduce-scatter.31.cloned.1.call-done = f32[256,2048]{1,0:T(8,128)} async-done(((f32[1024,2048]{1,0:T(8,128)}), f32[256,2048]{1,0:T(8,128)}) %reduce-scatter.31.cloned.1.call-update) | async-done | bytes 2097168 | tf_op jit(solution)/shard_map/reduce_scatter | solution.py:532
  1456.2 147.5 %reduce-scatter.35.cloned.1.call-done = f32[512,1024]{1,0:T(8,128)} async-done(((f32[2048,1024]{1,0:T(8,128)}), f32[512,1024]{1,0:T(8,128)}) %reduce-scatter.35.cloned.1.call-update) | async-done | bytes 2097168 | tf_op jit(solution)/shard_map/reduce_scatter | solution.py:534
  1603.8 232.0 %reduce-scatter.25.cloned.1.call-done = f32[256,3328]{1,0:T(8,128)} async-done(((f32[1024,3328]{1,0:T(8,128)}), f32[256,3328]{1,0:T(8,128)}) %reduce-scatter.25.cloned.1.call-update) | async-done | bytes 3407888 | tf_op jit(solution)/shard_map/reduce_scatter | solution.py:522
  1850.6 8.7 fusion.89
  1859.3 18.8 all-reduce.27
  1886.0 24.2 %all-reduce.25 = (f32[256]{0:T(256)}, f32[256,24]{0,1:T(8,128)}, f32[4,448]{1,0:T(4,128)}, f32[448]{0:T(512)}, f32[6]{0:T(128)}, /*index=5*/f32[6]{0:T(128)}, f32[6]{0:T(128)}, f32[384]{0:T(512)}, f32[256]{0:T(256)}) all-reduce(f32[256]{0:T(256)S(1)} %dynamic-slice.14, ...), channel_id=1, replica_groups=mesh['fsdp'=4,'ctx'=8] {'ctx'}, use_global_device_ids=true, to_apply=%region_35.36 | all-reduce | flops 9298 | bytes 74384 | tf_op jit(solution)/shard_map/psum | solution.py:556
  1910.2 155.0 %all-reduce.31.cloned.1.call-done = (f32[256,512]{1,0:T(8,128)}, f32[256,128]{1,0:T(8,128)}, f32[256,128]{1,0:T(8,128)}, f32[128,1024]{1,0:T(8,128)}, f32[256,33...) async-done(((f32[256,512]{1,0:T(8,128)}, f32[256,128]{1,0:T(8,128)}, f32[256,128]{1,0:T(8,128)}, ...) | async-done | bytes 12582928 | tf_op jit(solution)/shard_map/psum | solution.py:556
  (628 shorter events, 354.8 us)
Async XLA Ops:
  7.2 137.7 %all-gather.26.cloned.1.call-start = ((), (), s32[]{:S(2)}) async-start(), calls=%async_computation.16 | async-start | bytes 8519680 | tf_op jit(solution)/shard_map/all_gather | solution.py:247
  7.9 201.9 %all-gather.22.cloned.1.call-start = ((), (), s32[]{:S(2)}) async-start(), calls=%async_computation.14 | async-start | bytes 1310720 | tf_op jit(solution)/shard_map/all_gather | solution.py:243
  8.7 206.3 %all-gather.20.cloned.1.call-start = ((), (), s32[]{:S(2)}) async-start(), calls=%async_computation.13 | async-start | bytes 1179648 | tf_op jit(solution)/shard_map/all_gather | solution.py:315
  22.0 41.8 %copy-start.100 = (f32[4,1,256]{2,1,0:T(1,128)}, f32[4,1,256]{2,1,0:T(1,128)S(1)}, u32[]{:S(2)}) copy-start(f32[4,1,256]{2,1,0:T(1,128)S(1)} %convert_element_type.217) | copy-start | bytes 12292
  42.8 169.3 %copy-start.5 = (bf16[2,256,1024]{2,1,0:T(8,128)(2,1)}, bf16[2,256,1024]{2,1,0:T(8,128)(2,1)S(1)}, u32[]{:S(2)}) copy-start(bf16[2,256,1024]{2,1,0:T(8,128)(2,1)S(1)} %fusion.92) | copy-start | bytes 3145732
  42.9 48.2 %copy-start.134 = (bf16[256,24]{0,1:T(8,128)(2,1)S(1)}, bf16[256,24]{0,1:T(8,128)(2,1)}, u32[]{:S(2)}) copy-start(bf16[256,24]{0,1:T(8,128)(2,1)} %param.40) | copy-start | bytes 36868
  44.1 69.1 %copy-start.61 = (s32[2,2048]{1,0:T(2,128)S(1)}, s32[2,2048]{1,0:T(2,128)}, u32[]{:S(2)}) copy-start(s32[2,2048]{1,0:T(2,128)} %param.33) | copy-start | bytes 49156
  44.2 180.5 %all-gather.18.cloned.1.call-start = ((), (), s32[]{:S(2)}) async-start(), calls=%async_computation.12 | async-start | bytes 1179648 | tf_op jit(solution)/shard_map/all_gather | solution.py:316
  44.2 70.2 %copy-start.123 = (f32[1,2,2,128]{3,1,2,0:T(2,128)}, f32[1,2,2,128]{3,1,2,0:T(2,128)S(1)}, u32[]{:S(2)}) copy-start(f32[1,2,2,128]{3,1,2,0:T(2,128)S(1)} %copy.257) | copy-start | bytes 6148
  44.2 70.2 %copy-start.119 = (f32[512]{0:T(512)}, f32[512]{0:T(512)S(1)}, u32[]{:S(2)}) copy-start(f32[512]{0:T(512)S(1)} %rsqrt.36) | copy-start | bytes 6148
  65.4 233.8 %all-gather.36.cloned.1.call-start = ((), (), s32[]{:S(2)}) async-start(), calls=%async_computation.32 | async-start | bytes 14155776 | tf_op jit(solution)/shard_map/all_gather | solution.py:33
  111.6 39.5 %copy-start.57 = (f32[2,256,24]{1,2,0:T(8,128)}, f32[2,256,24]{1,2,0:T(8,128)S(1)}, u32[]{:S(2)}) copy-start(f32[2,256,24]{1,2,0:T(8,128)S(1)} %get-tuple-element.627) | copy-start | bytes 147460
  111.6 39.5 %copy-start.88 = (u8[256,24]{0,1:T(8,128)(4,1)}, u8[256,24]{0,1:T(8,128)(4,1)S(1)}, u32[]{:S(2)}) copy-start(u8[256,24]{0,1:T(8,128)(4,1)S(1)} %get-tuple-element.470) | copy-start | bytes 18436
  112.8 38.3 %copy-start.40 = (f32[2,24,2,128]{3,1,2,0:T(8,128)}, f32[2,24,2,128]{3,1,2,0:T(8,128)S(1)}, u32[]{:S(2)}) copy-start(f32[2,24,2,128]{3,1,2,0:T(8,128)S(1)} %reduce-window.20) | copy-start | bytes 147460
  113.0 38.1 %copy-start.98 = (f32[2,24,2]{1,2,0:T(2,128)}, f32[2,24,2]{1,2,0:T(2,128)S(1)}, u32[]{:S(2)}) copy-start(f32[2,24,2]{1,2,0:T(2,128)S(1)} %slice.217) | copy-start | bytes 1156
  113.1 38.0 %copy-start.83 = (f32[2,256,24]{1,2,0:T(8,128)}, f32[2,256,24]{1,2,0:T(8,128)S(1)}, u32[]{:S(2)}) copy-start(f32[2,256,24]{1,2,0:T(8,128)S(1)} %bitcast_bitcast_fusion.1) | copy-start | bytes 147460
  113.7 40.3 %copy-start.127 = (pred[2,256]{1,0:T(4,128)(4,1)}, pred[2,256]{1,0:T(4,128)(4,1)S(1)}, u32[]{:S(2)}) copy-start(pred[2,256]{1,0:T(4,128)(4,1)S(1)} %get-tuple-element.613) | copy-start | bytes 1540
  113.7 40.3 %copy-start.129 = (pred[2,256]{1,0:T(4,128)(4,1)}, pred[2,256]{1,0:T(4,128)(4,1)S(1)}, u32[]{:S(2)}) copy-start(pred[2,256]{1,0:T(4,128)(4,1)S(1)} %get-tuple-element.614) | copy-start | bytes 1540
  113.7 40.3 %copy-start.131 = (pred[2,256]{1,0:T(4,128)(4,1)}, pred[2,256]{1,0:T(4,128)(4,1)S(1)}, u32[]{:S(2)}) copy-start(pred[2,256]{1,0:T(4,128)(4,1)S(1)} %get-tuple-element.615) | copy-start | bytes 1540
  114.5 52.2 %copy-start.71 = (f32[2,256,24]{1,2,0:T(8,128)}, f32[2,256,24]{1,2,0:T(8,128)S(1)}, u32[]{:S(2)}) copy-start(f32[2,256,24]{1,2,0:T(8,128)S(1)} %get-tuple-element.611) | copy-start | bytes 147460
  151.2 2.9 collective-permute-start
  172.5 191.5 %all-gather.28.cloned.1.call-start = ((), (), s32[]{:S(2)}) async-start(), calls=%async_computation.17 | async-start | bytes 3932160 | tf_op jit(solution)/shard_map/all_gather | solution.py:255
  173.1 219.1 %all-gather.24.cloned.1.call-start = ((), (), s32[]{:S(2)}) async-start(), calls=%async_computation.15 | async-start | bytes 1310720 | tf_op jit(solution)/shard_map/all_gather | solution.py:246
  173.9 300.3 %all-gather.32.cloned.1.call-start = ((), (), s32[]{:S(2)}) async-start(), calls=%async_computation.19 | async-start | bytes 5242880 | tf_op jit(solution)/shard_map/all_gather | solution.py:258
  174.6 380.4 %all-gather.30.cloned.1.call-start = ((), (), s32[]{:S(2)}) async-start(), calls=%async_computation.18 | async-start | bytes 5242880 | tf_op jit(solution)/shard_map/all_gather | solution.py:257
  175.3 460.4 %all-gather.34.cloned.1.call-start = ((), (), s32[]{:S(2)}) async-start(), calls=%async_computation.20 | async-start | bytes 5242880 | tf_op jit(solution)/shard_map/all_gather | solution.py:259
  175.9 661.1 %reduce-scatter.15.cloned.1.call-start = ((), (), s32[]{:S(2)}) async-start(), calls=%async_computation.21 | async-start | bytes 4718592 | tf_op jit(solution)/shard_map/reduce_scatter | solution.py:478
  184.9 131.1 %copy-start.150 = (f32[24]{0:T(128)}, f32[24]{0:T(128)S(1)}, u32[]{:S(2)}) copy-start(f32[24]{0:T(128)S(1)} %convert_element_type.193) | copy-start | bytes 292
  197.6 118.5 %copy-start.86 = (pred[2,256,256]{2,1,0:T(8,128)(4,1)}, pred[2,256,256]{2,1,0:T(8,128)(4,1)S(1)}, u32[]{:S(2)}) copy-start(pred[2,256,256]{2,1,0:T(8,128)(4,1)S(1)} %compare_and_fusion) | copy-start | bytes 393220
  272.3 43.7 %copy-start.68 = (f32[2,256,256]{2,1,0:T(8,128)}, f32[2,256,256]{2,1,0:T(8,128)S(1)}, u32[]{:S(2)}) copy-start(f32[2,256,256]{2,1,0:T(8,128)S(1)} %fusion.129) | copy-start | bytes 1572868
  395.2 256.5 %copy-start.15 = (f32[512,1024]{1,0:T(8,128)}, f32[512,1024]{1,0:T(8,128)S(1)}, u32[]{:S(2)}) copy-start(f32[512,1024]{1,0:T(8,128)S(1)} %get-tuple-element.629) | copy-start | bytes 6291460
  395.2 256.5 %copy-start.115 = (f32[512]{0:T(512)}, f32[512]{0:T(512)S(1)}, u32[]{:S(2)}) copy-start(f32[512]{0:T(512)S(1)} %fusion.159) | copy-start | bytes 6148
  395.5 78.6 %copy-start.62 = (bf16[512,1024]{1,0:T(8,128)(2,1)}, bf16[512,1024]{1,0:T(8,128)(2,1)S(1)}, u32[]{:S(2)}) copy-start(bf16[512,1024]{1,0:T(8,128)(2,1)S(1)} %multiply_convert_fusion.3) | copy-start | bytes 3145732
  480.6 155.2 %copy-start.35 = (bf16[2,256,1024]{2,1,0:T(8,128)(2,1)S(1)}, bf16[2,256,1024]{2,1,0:T(8,128)(2,1)}, u32[]{:S(2)}) copy-start(bf16[2,256,1024]{2,1,0:T(8,128)(2,1)} %param.32) | copy-start | bytes 3145732
  787.1 124.6 %all-gather.38.cloned.1.call-start = ((), (), s32[]{:S(2)}) async-start(), calls=%async_computation.33 | async-start | bytes 14155776 | tf_op jit(solution)/shard_map/all_gather | solution.py:33
  807.2 217.1 %reduce-scatter.23.cloned.1.call-start = ((), (), s32[]{:S(2)}) async-start(), calls=%async_computation.25 | async-start | bytes 2621440 | tf_op jit(solution)/shard_map/reduce_scatter | solution.py:521
  811.2 213.0 %reduce-scatter.17.cloned.1.call-start = ((), (), s32[]{:S(2)}) async-start(), calls=%async_computation.22 | async-start | bytes 2621440 | tf_op jit(solution)/shard_map/reduce_scatter | solution.py:518
  816.1 211.6 %reduce-scatter.19.cloned.1.call-start = ((), (), s32[]{:S(2)}) async-start(), calls=%async_computation.23 | async-start | bytes 655360 | tf_op jit(solution)/shard_map/reduce_scatter | solution.py:519
  839.8 210.1 %reduce-scatter.21.cloned.1.call-start = ((), (), s32[]{:S(2)}) async-start(), calls=%async_computation.24 | async-start | bytes 655360 | tf_op jit(solution)/shard_map/reduce_scatter | solution.py:520
  841.2 320.0 %reduce-scatter.29.cloned.1.call-start = ((), (), s32[]{:S(2)}) async-start(), calls=%async_computation.28 | async-start | bytes 7864320 | tf_op jit(solution)/shard_map/reduce_scatter | solution.py:530
  847.4 461.1 %reduce-scatter.33.cloned.1.call-start = ((), (), s32[]{:S(2)}) async-start(), calls=%async_computation.30 | async-start | bytes 10485760 | tf_op jit(solution)/shard_map/reduce_scatter | solution.py:533
  855.3 601.0 %reduce-scatter.31.cloned.1.call-start = ((), (), s32[]{:S(2)}) async-start(), calls=%async_computation.29 | async-start | bytes 10485760 | tf_op jit(solution)/shard_map/reduce_scatter | solution.py:532
  862.5 741.2 %reduce-scatter.35.cloned.1.call-start = ((), (), s32[]{:S(2)}) async-start(), calls=%async_computation.31 | async-start | bytes 10485760 | tf_op jit(solution)/shard_map/reduce_scatter | solution.py:534
  870.2 965.6 %reduce-scatter.25.cloned.1.call-start = ((), (), s32[]{:S(2)}) async-start(), calls=%async_computation.26 | async-start | bytes 17039360 | tf_op jit(solution)/shard_map/reduce_scatter | solution.py:522
  975.7 8.0 collective-permute-start.1
  996.4 887.2 %reduce-scatter.37.cloned.1.call-start = ((), (), s32[]{:S(2)}) async-start(), calls=%async_computation.34 | async-start | bytes 1146880
  1021.8 864.1 %reduce-scatter.27.cloned.1.call-start = ((), (), s32[]{:S(2)}) async-start(), calls=%async_computation.27 | async-start | bytes 122880 | tf_op jit(solution)/shard_map/reduce_scatter | solution.py:523
  1023.9 1041.3 %all-reduce.31.cloned.1.call-start = ((), (), s32[]{:S(2)}) async-start(), calls=%async_computation.35 | async-start | bytes 25165824 | tf_op jit(solution)/shard_map/psum | solution.py:556
  (137 other events, 1223.2 us)
Sparse Core Ops, SparseCore 0:
  9.6 135.2 all-gather.25
  146.5 26.6 all-gather.21
  175.6 23.0 all-gather.19
  201.0 23.5 all-gather.17
  227.0 72.1 all-gather.35
  300.5 63.4 all-gather.27
  365.6 26.5 all-gather.23
  393.8 80.2 all-gather.31
  475.7 79.2 all-gather.29
  556.4 79.2 all-gather.33
  787.2 49.8 reduce-scatter.14
  839.5 72.1 all-gather.37
  914.7 43.8 reduce-scatter.22
  961.3 43.1 reduce-scatter.16
  1006.7 20.9 reduce-scatter.18
  1030.0 19.8 reduce-scatter.20
  1052.2 108.9 reduce-scatter.28
  1163.5 144.9 reduce-scatter.32
  1311.0 145.1 reduce-scatter.30
  1458.6 145.1 reduce-scatter.34
  1606.3 229.4 reduce-scatter.24
  1838.8 26.1 reduce-scatter.36
  1867.9 18.0 reduce-scatter.26
  1891.1 174.0 all-reduce.30
where the time goes:
time: 2100 us; the launch traced here: 2090 us
  waiting for transfers between devices  1340 us (64%)
  matrix products  317 us (15%)
  blocking collectives  169 us (8%)
  other arithmetic  136 us (6%)
  local copies, waits for them, and re-layouts  104 us (5%)
  between operations  21.1 us (1%)
    reduce_scatter x1, waiting for transfers between devices, per_device(): lax.psum_scatter(mixer_grad, 'fsdp', scatter_dimension=0, tiled=True)  232 us
    psum x1, waiting for transfers between devices, per_device(): lax.psum((entry_part, query_part, key_part, value_part, output_part, mixe...  155 us
    reduce_scatter x1, waiting for transfers between devices, per_device(): lax.psum_scatter(gate_grad, 'fsdp', scatter_dimension=0, tiled=True)  148 us
    reduce_scatter x1, waiting for transfers between devices, per_device(): lax.psum_scatter(down_grad, 'fsdp', scatter_dimension=0, tiled=True)  148 us
    reduce_scatter x1, waiting for transfers between devices, per_device(): lax.psum_scatter(up_grad, 'fsdp', scatter_dimension=0, tiled=True)  147 us
    reduce_scatter x1, waiting for transfers between devices, per_device(): lax.psum_scatter(merge_grad, 'fsdp', scatter_dimension=0, tiled=True)  111 us
    all_gather x1, waiting for transfers between devices, per_device(): lax.all_gather(up_weight, 'fsdp', axis=0, tiled=True)  78.6 us
    all_gather x1, waiting for transfers between devices, per_device(): lax.all_gather(gate_weight, 'fsdp', axis=0, tiled=True)  74.4 us
  transfers between devices with their start and end apart: 26, of which 19 were waited for; matrix products, arithmetic and copies ran while one was open for 18% of the time, Pallas kernels for 0%

commit v1 on v0

v1 whole, which is shorter than its diff:
```python
import jax
import jax.numpy as jnp
from jax import lax
from jax.experimental import pallas as pl
from jax.experimental.pallas import tpu as pltpu
from jax.sharding import PartitionSpec as P

QHEADS = 8
KVHEADS = 2
HEAD = 64
MHEADS = 24
MHEAD = 64
STATE = 128
CONVW = 4
QW = 512
KW = 128
DS = 1536
PROJ = 3328


EPSILON = 1e-05
ROPE_BASE = 10000.0
SCORE_SCALE = 0.125
PRECISE = lax.Precision.HIGH
LANES = 128
VMEM_BYTES = 48 * 1024 * 1024


def shifted(block, axis, distance):
    devices = range(lax.axis_size(axis))
    route = [(i - distance, i) for i in devices if i - distance in devices]
    return lax.ppermute(block, axis, route)


def states_before(through_all, states_all, axis):
    count, mine = (states_all.shape[0], lax.axis_index(axis))
    order = jnp.arange(count)
    between = (order[None, :] > order[:, None]) & (order[None, :] < mine)
    factors = jnp.where(between[:, :, None, None], through_all[None], 1.0)
    weights = jnp.where((order < mine)[:, None, None], jnp.prod(factors, axis=1), 0.0)
    return jnp.sum(weights[..., None, None] * states_all.astype(jnp.float32), axis=0)


def states_after(through_all, states_all, axis):
    count, mine = (states_all.shape[0], lax.axis_index(axis))
    order = jnp.arange(count)
    between = (order[None, :] < order[:, None]) & (order[None, :] > mine)
    factors = jnp.where(between[:, :, None, None], through_all[None], 1.0)
    weights = jnp.where((order > mine)[:, None, None], jnp.prod(factors, axis=1), 0.0)
    return jnp.sum(weights[..., None, None] * states_all.astype(jnp.float32), axis=0)


def matmul(left, right):
    return jnp.dot(left, right, preferred_element_type=jnp.float32)


def weight_grad(left, right):
    return jnp.einsum("rd,rf->df", left, right, preferred_element_type=jnp.float32)


def back_product(grads_in, weight):
    return jnp.einsum("rf,df->rd", grads_in, weight, preferred_element_type=jnp.float32)


def root_norm(values, gain):
    return values * lax.rsqrt(jnp.mean(values * values, axis=-1, keepdims=True) + EPSILON) * gain


def rotate(heads, places):
    half_dim = heads.shape[-1] // 2
    freqs = ROPE_BASE ** (-2.0 * jnp.arange(half_dim, dtype=jnp.float32) / heads.shape[-1])
    angles = places.astype(jnp.float32)[:, None] * freqs[None, :]
    cosine = jnp.cos(angles)[:, None, :]
    sine = jnp.sin(angles)[:, None, :]
    front = heads[..., :half_dim]
    behind = heads[..., half_dim:]
    return jnp.concatenate(
        [front * cosine - behind * sine, behind * cosine + front * sine], axis=-1
    )


def block_decays(log_decay, segment):
    cumulate = jnp.cumsum(log_decay, axis=0)
    ordinal = jnp.arange(segment.shape[0], dtype=jnp.int32)
    related = (segment[:, None] == segment[None, :]) & (ordinal[:, None] >= ordinal[None, :])
    log_gap = jnp.where(related[:, :, None], cumulate[:, None, :] - cumulate[None, :, :], 0.0)
    return (cumulate, jnp.where(related[:, :, None], jnp.exp(log_gap), 0.0))


def block_state(ssm_input, in_matrix, step_size, log_decay, segment, prior_segment):
    cumulate = jnp.cumsum(log_decay, axis=0)
    tail_decay = (
        jnp.where((segment == segment[-1])[:, None], jnp.exp(cumulate[-1][None, :] - cumulate), 0.0)
        * step_size
    )
    local_state = jnp.einsum("jh,jhp,jn->hpn", tail_decay, ssm_input, in_matrix, precision=PRECISE)
    through = jnp.where(segment[-1] == prior_segment, jnp.exp(cumulate[-1]), 0.0)
    return (through, local_state)


def block_output(
    ssm_state, ssm_input, in_matrix, out_matrix, step_size, log_decay, segment, prior_segment
):
    cumulate, decays = block_decays(log_decay, segment)
    intersection = jnp.dot(out_matrix, in_matrix.T, precision=PRECISE)
    mixing = decays * intersection[:, :, None] * step_size[None, :, :]
    result = jnp.einsum("ijh,jhp->ihp", mixing, ssm_input, precision=PRECISE)
    carry_in = jnp.where((segment == prior_segment)[:, None], jnp.exp(cumulate), 0.0)
    return result + carry_in[:, :, None] * jnp.einsum(
        "in,hpn->ihp", out_matrix, ssm_state, precision=PRECISE
    )


def mamba_front(
    projected,
    rim_rows,
    step_raw,
    segment_ext,
    prior_segment,
    conv_taps,
    conv_shift,
    step_shift,
    decay_speed,
):
    length = projected.shape[0]
    back_reach = CONVW - 1
    conv_input = jnp.concatenate([rim_rows, projected[:, DS:]], axis=0)
    segment = segment_ext[back_reach:]
    summed = conv_input[back_reach:] * conv_taps[back_reach]
    for offset in range(1, CONVW):
        start_row = back_reach - offset
        earlier = conv_input[start_row : start_row + length]
        related = segment_ext[start_row : start_row + length] == segment
        summed = summed + jnp.where(related[:, None], earlier, 0.0) * conv_taps[start_row]
    activated = jax.nn.silu(summed + conv_shift)
    ssm_input = activated[:, :DS].reshape(length, MHEADS, MHEAD)
    in_matrix = activated[:, DS : DS + STATE]
    out_matrix = activated[:, DS + STATE :]
    step_size = jax.nn.softplus(step_raw + step_shift)
    log_decay = -step_size * decay_speed
    chain = block_state(ssm_input, in_matrix, step_size, log_decay, segment, prior_segment)
    return ((ssm_input, in_matrix, out_matrix, step_size, log_decay), chain)


def mamba_tail(ssm_state, inside, mixer_gate, segment, prior_segment, skip_scale, gated_scale):
    ssm_input, in_matrix, out_matrix, step_size, log_decay = inside
    length = mixer_gate.shape[0]
    ssm_out = (
        block_output(
            ssm_state,
            ssm_input,
            in_matrix,
            out_matrix,
            step_size,
            log_decay,
            segment,
            prior_segment,
        )
        + skip_scale[None, :, None] * ssm_input
    )
    gated_out = ssm_out.reshape(length, DS) * jax.nn.silu(mixer_gate)
    return root_norm(gated_out, gated_scale)


def dot_nn(left, right):
    return jnp.dot(left, right, preferred_element_type=jnp.float32)


def dot_nt(left, right):
    return lax.dot_general(
        left, right, (((1,), (1,)), ((), ())), preferred_element_type=jnp.float32
    )


def masked_scores(key_ref, query_ref, low_ref, high_ref):
    raw_scores = dot_nt(key_ref[0, 0], query_ref[0, 0]) * SCORE_SCALE
    places = lax.broadcasted_iota(jnp.int32, raw_scores.shape, 0)
    allowed = (places >= low_ref[0]) & (places <= high_ref[0])
    return jnp.where(allowed, raw_scores, -1e30)


def attend_forward_kernel(
    low_ref, high_ref, query_ref, key_ref, value_t_ref, out_ref, highest_ref, total_ref
):
    masked = masked_scores(key_ref, query_ref, low_ref, high_ref)
    highest = jnp.max(masked, axis=0, keepdims=True)
    weights = jnp.exp(masked - highest)
    total = jnp.sum(weights, axis=0, keepdims=True)
    probability = (weights * (1.0 / total)).astype(jnp.bfloat16)
    out_ref[0, 0] = dot_nn(value_t_ref[0, 0], probability)
    highest_ref[0, 0] = highest
    total_ref[0, 0] = total


def attend_backward_kernel(
    group_size,
    low_ref,
    high_ref,
    query_ref,
    delta_ref,
    key_ref,
    value_ref,
    key_t_ref,
    highest_ref,
    total_ref,
    centre_ref,
    query_out,
    key_out,
    value_out,
):
    masked = masked_scores(key_ref, query_ref, low_ref, high_ref)
    probability = jnp.exp(masked - highest_ref[0, 0]) * (1.0 / total_ref[0, 0])
    weight_delta = dot_nt(value_ref[0, 0], delta_ref[0, 0])
    score_low = (probability * (weight_delta - centre_ref[0, 0])).astype(jnp.bfloat16)
    query_out[0, 0] = dot_nn(key_t_ref[0, 0], score_low) * SCORE_SCALE
    key_term = dot_nn(score_low, query_ref[0, 0]) * SCORE_SCALE
    value_term = dot_nn(probability.astype(jnp.bfloat16), delta_ref[0, 0])
    first = pl.program_id(1) % group_size == 0

    @pl.when(first)
    def _():
        key_out[0, 0] = key_term
        value_out[0, 0] = value_term

    @pl.when(jnp.logical_not(first))
    def _():
        key_out[0, 0] += key_term
        value_out[0, 0] += value_term


def head_specs(batches, length, seq_span):
    group_size = QHEADS // KVHEADS
    return {
        "low": pl.BlockSpec((1, 1, length), lambda b, h: (b, 0, 0)),
        "high": pl.BlockSpec((1, 1, length), lambda b, h: (0, 0, 0)),
        "query": pl.BlockSpec((1, 1, length, HEAD), lambda b, h: (b, h, 0, 0)),
        "query_t": pl.BlockSpec((1, 1, HEAD, length), lambda b, h: (b, h, 0, 0)),
        "row": pl.BlockSpec((1, 1, 1, length), lambda b, h: (b, h, 0, 0)),
        "key": pl.BlockSpec((1, 1, seq_span, HEAD), lambda b, h: (b, h // group_size, 0, 0)),
        "key_t": pl.BlockSpec((1, 1, HEAD, seq_span), lambda b, h: (b, h // group_size, 0, 0)),
    }


def attend_forward(low, high, query_heads, key_heads, value_heads_t):
    batches, _, length, _ = query_heads.shape
    seq_span = key_heads.shape[2]
    specs = head_specs(batches, length, seq_span)
    return pl.pallas_call(
        attend_forward_kernel,
        grid=(batches, QHEADS),
        in_specs=[specs[name] for name in ("low", "high", "query", "key", "key_t")],
        out_specs=[specs["query_t"], specs["row"], specs["row"]],
        out_shape=[
            jax.ShapeDtypeStruct((batches, QHEADS, HEAD, length), jnp.float32),
            jax.ShapeDtypeStruct((batches, QHEADS, 1, length), jnp.float32),
            jax.ShapeDtypeStruct((batches, QHEADS, 1, length), jnp.float32),
        ],
        compiler_params=pltpu.CompilerParams(vmem_limit_bytes=VMEM_BYTES),
        cost_estimate=pl.CostEstimate(
            flops=8 * batches * QHEADS * length * seq_span * HEAD,
            bytes_accessed=24 * batches * seq_span * LANES,
            transcendentals=batches * QHEADS * length * seq_span,
        ),
    )(low, high, query_heads, key_heads, value_heads_t)


def attend_backward(
    low, high, query_heads, delta_heads, key_heads, value_heads, key_heads_t, highest, total, centre
):
    batches, _, length, _ = query_heads.shape
    seq_span = key_heads.shape[2]
    specs = head_specs(batches, length, seq_span)
    names = ("low", "high", "query", "query", "key", "key", "key_t", "row", "row", "row")

    def kernel(*refs):
        attend_backward_kernel(QHEADS // KVHEADS, *refs)

    return pl.pallas_call(
        kernel,
        grid=(batches, QHEADS),
        in_specs=[specs[name] for name in names],
        out_specs=[specs["query_t"], specs["key"], specs["key"]],
        out_shape=[
            jax.ShapeDtypeStruct((batches, QHEADS, HEAD, length), jnp.float32),
            jax.ShapeDtypeStruct((batches, KVHEADS, seq_span, HEAD), jnp.float32),
            jax.ShapeDtypeStruct((batches, KVHEADS, seq_span, HEAD), jnp.float32),
        ],
        compiler_params=pltpu.CompilerParams(vmem_limit_bytes=VMEM_BYTES),
        cost_estimate=pl.CostEstimate(
            flops=20 * batches * QHEADS * length * seq_span * HEAD,
            bytes_accessed=48 * batches * seq_span * LANES,
            transcendentals=batches * QHEADS * length * seq_span,
        ),
    )(
        low,
        high,
        query_heads,
        delta_heads,
        key_heads,
        value_heads,
        key_heads_t,
        highest,
        total,
        centre,
    )


def gather_rows(*shards):
    count, mine = (lax.axis_size("ctx"), lax.axis_index("ctx"))
    pieces = [
        lax.dynamic_slice_in_dim(shard, mine * (shard.shape[0] // count), shard.shape[0] // count, 0)
        for shard in shards
    ]
    width = sum(piece.shape[1] for piece in pieces)
    if width % LANES:
        pieces.append(jnp.zeros((pieces[0].shape[0], LANES - width % LANES), pieces[0].dtype))
    joined = jnp.concatenate(pieces, axis=1) if len(pieces) > 1 else pieces[0]
    return lax.all_gather(joined, ("fsdp", "ctx"), axis=0, tiled=True)


def reduce_rows(grads):
    splits, count = (lax.axis_size("fsdp"), lax.axis_size("ctx"))
    blocks = [
        grad.astype(jnp.bfloat16).reshape(splits, count, -1, grad.shape[1]) for grad in grads
    ]
    heights = [block.shape[2] for block in blocks]
    joined = jnp.concatenate(blocks, axis=2) if len(blocks) > 1 else blocks[0]
    width = joined.shape[3]
    joined = joined.transpose(1, 0, 2, 3).reshape(-1, width)
    part = lax.psum_scatter(joined, "ctx", scatter_dimension=0, tiled=True)
    part = lax.psum_scatter(part, "fsdp", scatter_dimension=0, tiled=True)
    rows = lax.all_gather(part, "ctx", axis=0, tiled=True)
    rows = rows.reshape(count, -1, width)
    results, at = ([], 0)
    for height in heights:
        results.append(rows[:, at : at + height].reshape(-1, width).astype(jnp.float32))
        at += height
    return results


def per_device(
    hidden_in,
    cotangent,
    segments,
    entry_gain,
    query_weight,
    key_weight,
    value_weight,
    output_weight,
    mixer_weight,
    step_weight,
    conv_weight,
    conv_bias,
    step_offset,
    decay_rate,
    skip_weight,
    gated_gain,
    merge_weight,
    second_gain,
    gate_weight,
    up_weight,
    down_weight,
):
    splits = lax.axis_size("fsdp")
    narrow = (
        entry_gain,
        conv_weight.reshape(-1),
        conv_bias,
        step_offset,
        decay_rate,
        skip_weight,
        gated_gain,
        second_gain,
    )
    narrow_all = lax.all_gather(jnp.concatenate(narrow), "fsdp", axis=0)
    wide = []
    at = 0
    for piece in narrow:
        wide.append(narrow_all[:, at : at + piece.shape[0]].astype(jnp.float32))
        at += piece.shape[0]
    entry_scale, conv_shift, step_shift, decay_speed, skip_scale, gated_scale, second_scale = [
        wide[i].reshape(-1) for i in (0, 2, 3, 4, 5, 6, 7)
    ]
    conv_taps = wide[1].reshape(splits, CONVW, -1).transpose(1, 0, 2).reshape(CONVW, -1)
    front_full = gather_rows(query_weight, key_weight, value_weight, mixer_weight, step_weight)
    output_full = gather_rows(output_weight)
    merge_full = gather_rows(merge_weight)
    rise_full = gather_rows(gate_weight, up_weight)
    down_full = gather_rows(down_weight)
    batches, length, features = hidden_in.shape
    flat_rows = batches * length
    back_reach = CONVW - 1
    first_proj = QW + 2 * KW
    first_step = first_proj + PROJ
    anchor = lax.axis_index("ctx") * length
    places = anchor + jnp.arange(length, dtype=jnp.int32)
    padded_segments = jnp.concatenate(
        [jnp.full((batches, back_reach), -1, jnp.int32), segments], axis=1
    )
    segment_ext = lax.dynamic_slice_in_dim(padded_segments, anchor, length + back_reach, 1)
    segment_here = segment_ext[:, back_reach:]
    prior_segment = segment_ext[:, back_reach - 1]
    document_start = jnp.sum(
        (segments[:, None, :] < segment_here[:, :, None]).astype(jnp.int32), axis=2
    )[:, None, :]
    place_row = places[None, None, :]
    tokens = hidden_in.reshape(flat_rows, features).astype(jnp.float32)
    normed = root_norm(tokens, entry_scale).astype(jnp.bfloat16)
    front = matmul(normed, front_full)

    def split_heads(rows, count):
        return rows.reshape(batches, -1, count, HEAD).transpose(0, 2, 1, 3)

    queries = split_heads(
        rotate(front[:, :QW].reshape(batches, length, QHEADS, HEAD), places).astype(jnp.bfloat16),
        QHEADS,
    )
    key_rows = (
        rotate(front[:, QW : QW + KW].reshape(batches, length, KVHEADS, HEAD), places)
        .astype(jnp.bfloat16)
        .reshape(batches, length, KW)
    )
    value_rows = front[:, QW + KW : first_proj].astype(jnp.bfloat16).reshape(batches, length, KW)
    all_pairs = lax.all_gather(
        jnp.concatenate([key_rows, value_rows], axis=2), "ctx", axis=1, tiled=True
    )
    key_heads = split_heads(all_pairs[:, :, :KW], KVHEADS)
    value_heads = split_heads(all_pairs[:, :, KW:], KVHEADS)
    attended_t, highest, total = attend_forward(
        document_start, place_row, queries, key_heads, value_heads.swapaxes(2, 3)
    )
    attended_low = (
        attended_t.astype(jnp.bfloat16).transpose(0, 3, 1, 2).reshape(flat_rows, QW)
    )
    projected = front[:, first_proj:first_step].reshape(batches, length, PROJ)
    step_raw = front[:, first_step : first_step + MHEADS].reshape(batches, length, MHEADS)
    rim_rows = shifted(projected[:, length - back_reach :, DS:], "ctx", 1)
    front_map = jax.vmap(mamba_front, in_axes=(0, 0, 0, 0, 0, None, None, None, None))
    tail_map = jax.vmap(mamba_tail, in_axes=(0, 0, 0, 0, 0, None, None))
    inside, chain = front_map(
        projected,
        rim_rows,
        step_raw,
        segment_ext,
        prior_segment,
        conv_taps,
        conv_shift,
        step_shift,
        decay_speed,
    )
    through_decay, local_state = chain
    through_all = lax.all_gather(through_decay, "ctx")
    state_in = states_before(
        through_all, lax.all_gather(local_state.astype(jnp.bfloat16), "ctx"), "ctx"
    )
    mixer_gate = projected[:, :, :DS]
    mixed = tail_map(
        state_in, inside, mixer_gate, segment_here, prior_segment, skip_scale, gated_scale
    )
    mixed_low = mixed.reshape(flat_rows, DS).astype(jnp.bfloat16)
    middle = tokens + matmul(attended_low, output_full) + matmul(mixed_low, merge_full)
    second = root_norm(middle, second_scale).astype(jnp.bfloat16)
    rise = matmul(second, rise_full)
    half = rise.shape[1] // 2
    gate_proj = rise[:, :half]
    up_proj = rise[:, half:]
    hidden = (jax.nn.silu(gate_proj) * up_proj).astype(jnp.bfloat16)
    block_out = (middle + matmul(hidden, down_full)).reshape(batches, length, features)
    incoming = cotangent.reshape(flat_rows, features)
    (down_sum,) = reduce_rows([weight_grad(hidden, incoming)])
    hidden_delta = back_product(incoming, down_full)
    _, swiglu_pull = jax.vjp(
        lambda gate_in, up_in: jax.nn.silu(gate_in) * up_in, gate_proj, up_proj
    )
    gate_delta, up_delta = swiglu_pull(hidden_delta)
    rise_low = jnp.concatenate([gate_delta, up_delta], axis=1).astype(jnp.bfloat16)
    (rise_sum,) = reduce_rows([weight_grad(second, rise_low)])
    gate_sum = rise_sum[:, :half]
    up_sum = rise_sum[:, half:]
    second_delta = back_product(rise_low, rise_full)
    _, second_pull = jax.vjp(root_norm, middle, second_scale)
    middle_norm_delta, second_grad = second_pull(second_delta)
    middle_delta = incoming.astype(jnp.float32) + middle_norm_delta
    branch_low = middle_delta.astype(jnp.bfloat16)
    output_sum, merge_sum = reduce_rows(
        [weight_grad(attended_low, branch_low), weight_grad(mixed_low, branch_low)]
    )
    attended_delta = back_product(branch_low, output_full).astype(jnp.bfloat16)
    mixed_delta = (
        lax.optimization_barrier(back_product(branch_low, merge_full).astype(jnp.bfloat16))
        .astype(jnp.float32)
        .reshape(batches, length, DS)
    )

    def tail_apply(state_value, inside_value, gate_value, skip_value, gain_value):
        return tail_map(
            state_value,
            inside_value,
            gate_value,
            segment_here,
            prior_segment,
            skip_value,
            gain_value,
        )

    _, tail_pull = jax.vjp(tail_apply, state_in, inside, mixer_gate, skip_scale, gated_scale)
    state_delta, inside_delta, gate_z_delta, skip_grad, gated_grad = tail_pull(mixed_delta)
    carried_delta = states_after(
        through_all, lax.all_gather(state_delta.astype(jnp.bfloat16), "ctx"), "ctx"
    )
    through_delta = jnp.sum(carried_delta * state_in, axis=(2, 3))

    def front_apply(
        proj_value, rim_value, step_value, taps_value, shift_value, offset_value, decay_value
    ):
        return front_map(
            proj_value,
            rim_value,
            step_value,
            segment_ext,
            prior_segment,
            taps_value,
            shift_value,
            offset_value,
            decay_value,
        )

    _, front_pull = jax.vjp(
        front_apply, projected, rim_rows, step_raw, conv_taps, conv_shift, step_shift, decay_speed
    )
    delta_heads = split_heads(attended_delta, QHEADS)
    centre = jnp.sum(
        attended_t * delta_heads.astype(jnp.float32).swapaxes(2, 3), axis=2, keepdims=True
    )
    query_delta_t, key_part, value_part = attend_backward(
        document_start,
        place_row,
        queries,
        delta_heads,
        key_heads,
        value_heads,
        key_heads.swapaxes(2, 3),
        highest,
        total,
        centre,
    )
    pair_delta = lax.psum_scatter(
        jnp.concatenate([key_part, value_part], axis=1)
        .astype(jnp.bfloat16)
        .transpose(2, 0, 1, 3)
        .reshape(-1, batches * 2 * KW),
        "ctx",
        scatter_dimension=0,
        tiled=True,
    )
    pair_delta = (
        pair_delta.astype(jnp.float32).reshape(length, batches, 2 * KW).swapaxes(0, 1)
    )
    key_low = (
        rotate(pair_delta[:, :, :KW].reshape(batches, length, KVHEADS, HEAD), -places)
        .astype(jnp.bfloat16)
        .reshape(flat_rows, KW)
    )
    value_low = pair_delta[:, :, KW:].astype(jnp.bfloat16).reshape(flat_rows, KW)
    query_low = (
        rotate(query_delta_t.transpose(0, 3, 1, 2), -places)
        .astype(jnp.bfloat16)
        .reshape(flat_rows, QW)
    )
    early_low = jnp.concatenate(
        [
            query_low,
            key_low,
            value_low,
            gate_z_delta.astype(jnp.bfloat16).reshape(flat_rows, DS),
        ],
        axis=1,
    )
    (early_sum,) = reduce_rows([weight_grad(normed, early_low)])
    query_sum = early_sum[:, :QW]
    key_sum = early_sum[:, QW : QW + KW]
    value_sum = early_sum[:, QW + KW : first_proj]
    proj_delta, rim_delta, step_delta, conv_grad, bias_grad, offset_grad, decay_grad = front_pull(
        (inside_delta, (through_delta, carried_delta))
    )
    rim_back = shifted(rim_delta, "ctx", -1)
    conv_delta = proj_delta[:, :, DS:].at[:, length - back_reach :].add(rim_back)
    late_low = jnp.concatenate(
        [
            conv_delta.reshape(flat_rows, PROJ - DS),
            step_delta.reshape(flat_rows, MHEADS),
            jnp.zeros((flat_rows, front_full.shape[1] - first_step - MHEADS), jnp.float32),
        ],
        axis=1,
    ).astype(jnp.bfloat16)
    (late_sum,) = reduce_rows([weight_grad(normed, late_low)])
    mixer_sum = jnp.concatenate([early_sum[:, first_proj:], late_sum[:, : PROJ - DS]], axis=1)
    step_sum = late_sum[:, PROJ - DS : PROJ - DS + MHEADS]
    early_width = early_low.shape[1]
    normed_delta = back_product(early_low, front_full[:, :early_width]) + back_product(
        late_low, front_full[:, early_width:]
    )
    _, entry_pull = jax.vjp(root_norm, tokens, entry_scale)
    token_delta, entry_grad = entry_pull(normed_delta)
    tokens_grad = (middle_delta + token_delta).reshape(batches, length, features)
    slight = (
        entry_grad,
        conv_grad.reshape(-1),
        bias_grad,
        offset_grad,
        decay_grad,
        skip_grad,
        gated_grad,
        second_grad,
    )
    slight_all = lax.psum(jnp.concatenate(slight), ("fsdp", "ctx"))
    sums = []
    at = 0
    for index, piece in enumerate(slight):
        whole = slight_all[at : at + piece.shape[0]]
        at += piece.shape[0]
        whole = whole.reshape((CONVW, -1) if index == 1 else (1, -1))
        share = whole.shape[1] // splits
        own = lax.dynamic_slice_in_dim(whole, lax.axis_index("fsdp") * share, share, 1)
        sums.append(own if index == 1 else own.reshape(-1))
    entry_sum, conv_sum, bias_sum, offset_sum, decay_sum, skip_sum, gated_sum, second_sum = sums
    return (
        block_out,
        tokens_grad,
        entry_sum,
        query_sum,
        key_sum,
        value_sum,
        output_sum,
        mixer_sum,
        step_sum,
        conv_sum,
        bias_sum,
        offset_sum,
        decay_sum,
        skip_sum,
        gated_sum,
        merge_sum,
        second_sum,
        gate_sum,
        up_sum,
        down_sum,
    )


def solution(mesh):
    placed = (
        P("fsdp", "ctx", None),
        P("fsdp", "ctx", None),
        P("fsdp", None),
        P("fsdp"),
        P("fsdp", None),
        P("fsdp", None),
        P("fsdp", None),
        P("fsdp", None),
        P("fsdp", None),
        P("fsdp", None),
        P(None, "fsdp"),
        P("fsdp"),
        P("fsdp"),
        P("fsdp"),
        P("fsdp"),
        P("fsdp"),
        P("fsdp", None),
        P("fsdp"),
        P("fsdp", None),
        P("fsdp", None),
        P("fsdp", None),
    )
    return jax.shard_map(
        per_device,
        mesh=mesh,
        in_specs=placed,
        out_specs=(
            P("fsdp", "ctx", None),
            P("fsdp", "ctx", None),
            P("fsdp"),
            P("fsdp", None),
            P("fsdp", None),
            P("fsdp", None),
            P("fsdp", None),
            P("fsdp", None),
            P("fsdp", None),
            P(None, "fsdp"),
            P("fsdp"),
            P("fsdp"),
            P("fsdp"),
            P("fsdp"),
            P("fsdp"),
            P("fsdp", None),
            P("fsdp"),
            P("fsdp", None),
            P("fsdp", None),
            P("fsdp", None),
        ),
        check_vma=False,
    )
```

time: 2100 us -> 1160 us (0.55)
  waiting for transfers between devices: 1340 us -> 596 us
  matrix products: 317 us -> 161 us
  blocking collectives: 169 us -> 83.8 us
  Pallas kernels: 0 us -> 61.6 us
  other arithmetic: 136 us -> 93.3 us
  local copies, waits for them, and re-layouts: 104 us -> 130 us
    reduce_scatter x11, waiting for transfers between devices: 834 us -> 269 us  [the longest x5 187 us: reduce_rows(): part = lax.psum_scatter(joined, 'ctx', scatter_dimension=0, tiled=True)]
    psum x1 -> x0, waiting for transfers between devices: 155 us -> none  [per_device(): lax.psum((entry_part, query_part, key_part, value_part, output_part, mixe...]
    all_gather x8 -> x2, blocking collectives: 117 us -> 22.4 us  [the longest x1 13.4 us: reduce_rows(): rows = lax.all_gather(part, 'ctx', axis=0, tiled=True)]
    dot_general x8 -> x0, matrix products: 69.6 us -> none  [the longest x2 28.3 us: attend_backward(): jnp.einsum('qgrd,kgd->grqk', delta_heads, value_heads, preferred_element_...]
    pallas_call x0 -> x2, Pallas kernels: none -> 61.6 us  [the longest x1 36.1 us: attend_backward(): pl.pallas_call(kernel, grid=(batches, QHEADS), in_specs=[specs[name] for...]
    sub x4 -> x0, matrix products: 41.9 us -> none  [score_weights(): weights = jnp.exp(masked - highest)]
    dynamic_update_slice x2 -> x0, other arithmetic: 35.5 us -> none  [per_device(): lax.map(lambda pieces: attend_backward(pieces, places), (queries, back_ke...]
    select_n x14 -> x3, other arithmetic: 25 us -> 0.85 us  [the longest x1 0.67 us: states_after(): jnp.where((order > mine)[:, None, None], jnp.prod(factors, axis=1), 0.0)]
  transfers between devices with their start and end apart: 26 -> 25, of which waited for: 19 -> 17; matrix products, arithmetic and copies ran while one was open for 18% -> 27% of each run, Pallas kernels for 0% -> 2%
where the time goes in v1:
time: 1160 us; the launch traced here: 1150 us
  waiting for transfers between devices  596 us (51%)
  matrix products  161 us (14%)
  local copies, waits for them, and re-layouts  130 us (11%)
  other arithmetic  93.3 us (8%)
  blocking collectives  83.8 us (7%)
  Pallas kernels  61.6 us (5%)
  between operations  17.1 us (1%)
    all_gather x5, waiting for transfers between devices, gather_rows(): return lax.all_gather(joined, ('fsdp', 'ctx'), axis=0, tiled=True)  246 us
    reduce_scatter x5, waiting for transfers between devices, reduce_rows(): part = lax.psum_scatter(joined, 'ctx', scatter_dimension=0, tiled=True)  187 us
    reduce_scatter x5, waiting for transfers between devices, reduce_rows(): part = lax.psum_scatter(part, 'fsdp', scatter_dimension=0, tiled=True)  74.9 us
    all_gather x1, waiting for transfers between devices, per_device(): lax.all_gather(state_delta.astype(jnp.bfloat16), 'ctx')  47.4 us
    psum x1, blocking collectives, per_device(): slight_all = lax.psum(jnp.concatenate(slight), ('fsdp', 'ctx'))  40.5 us
    dot_general x6, matrix products, back_product(): jnp.einsum('rf,df->rd', grads_in, weight, preferred_element_type=jnp.floa...  37.1 us
    pallas_call x1, Pallas kernels, attend_backward(): pl.pallas_call(kernel, grid=(batches, QHEADS), in_specs=[specs[name] for...  36.1 us
    dot_general x5, matrix products, matmul(): return jnp.dot(left, right, preferred_element_type=jnp.float32)  35.9 us
  transfers between devices with their start and end apart: 25, of which 17 were waited for; matrix products, arithmetic and copies ran while one was open for 27% of the time, Pallas kernels for 2%

profile of v1, /device:TPU:0, one launch (start us, length us, event | category | flops | bytes accessed | tf_op | source)
XLA Modules:
  0.0 1149.2 jit_solution(6619666057928212792)
XLA Ops:
  13.8 4.8 concatenate.62
  18.9 20.8 %all-reduce.14 = bf16[12616]{0:T(1024)(128)(2,1)S(1)} all-reduce(bf16[12616]{0:T(1024)(128)(2,1)S(1)} %dynamic-update-slice.3), channel_id=2, replica_groups=mesh['fsdp'=4,'ctx'=8] {'fsdp'}, use_global_device_ids=true, to_apply=%add.14 | all-reduce | flops 12616 | bytes 50464
  42.4 50.6 %all-gather.16.cloned.1.call-done = bf16[1024,4224]{1,0:T(8,128)(2,1)} async-done(((bf16[32,4224]{1,0:T(8,128)(2,1)}), bf16[1024,4224]{1,0:T(8,128)(2,1)}) %all-gather.16.cloned.1.call-update) | async-done | bytes 8650768 | tf_op jit(solution)/shard_map/all_gather | solution.py:318
  93.0 7.6 fusion.155
  107.8 6.3 slice.358
  122.8 4.8 fusion.42
  149.6 9.0 all_gather.60
  171.6 25.5 %shard_map.356 = (f32[2,8,64,256]{3,2,1,0:T(8,128)S(1)}, f32[2,8,1,256]{3,2,1,0:T(1,128)S(1)}, f32[2,8,1,256]{3,2,1,0:T(1,128)S(1)}) custom-call(s32[2,1,256]{2,1,0:T(1,128)S(1)} %broadcast_in_dim.278.low_ref.refs_0_, s32[1,1,256]{2,1,0:T(1,128)S(1)} %iota_add_fusion.1.high_ref.refs_1_, bf16[2,8,256,64]{3,2,1,0:T(8,128)(2,1)S(1)} %copy-done.3, ...), custom_call_target="tpu_custom_call" | custom-call | flops 4294967296 | bytes 12582912 | tf_op jit(solution)/shard_map/pallas_call | solution.py:248
  207.5 9.6 fusion.49
  228.0 17.3 %all-gather.22.cloned.1.call-done = bf16[1536,1024]{1,0:T(8,128)(2,1)} async-done(((bf16[48,1024]{1,0:T(8,128)(2,1)}), bf16[1536,1024]{1,0:T(8,128)(2,1)}) %all-gather.22.cloned.1.call-update) | async-done | bytes 3145744 | tf_op jit(solution)/shard_map/all_gather | solution.py:318
  245.4 5.6 fusion.156
  250.9 50.2 %all-gather.20.cloned.1.call-done = bf16[512,1024]{1,0:T(8,128)(2,1)} async-done(((bf16[16,1024]{1,0:T(8,128)(2,1)}), bf16[512,1024]{1,0:T(8,128)(2,1)}) %all-gather.20.cloned.1.call-update) | async-done | bytes 1048592 | tf_op jit(solution)/shard_map/all_gather | solution.py:318
  301.2 4.2 multiply_reduce_fusion.11
  305.4 75.5 %all-gather.24.cloned.1.call-done = bf16[1024,4096]{1,0:T(8,128)(2,1)} async-done(((bf16[32,4096]{1,0:T(8,128)(2,1)}), bf16[1024,4096]{1,0:T(8,128)(2,1)}) %all-gather.24.cloned.1.call-update) | async-done | bytes 8388624 | tf_op jit(solution)/shard_map/all_gather | solution.py:318
  380.9 12.0 %fusion.139 = f32[512,4096]{1,0:T(8,128)} fusion(bf16[1024,4096]{1,0:T(8,128)(2,1)} %all-gather.24.cloned.1.call-done, f32[512,1024]{1,0:T(8,128)} %get-tuple-element.257, f32[1024]{0:T(1024)S(1)} %bitcast.381, f32[512]{0:T(512)S(1)} %fusion.128), kind=kOutput, calls=%fused_computation.292 | convolution fusion | flops 4296540160 | bytes 18880512 | tf_op jit(solution)/shard_map/dot_general | solution.py:54
  392.9 52.1 %all-gather.26.cloned.1.call-done = bf16[2048,1024]{1,0:T(8,128)(2,1)} async-done(((bf16[64,1024]{1,0:T(8,128)(2,1)}), bf16[2048,1024]{1,0:T(8,128)(2,1)}) %all-gather.26.cloned.1.call-update) | async-done | bytes 4194320 | tf_op jit(solution)/shard_map/all_gather | solution.py:318
  445.0 9.3 fusion.28
  454.3 8.0 multiply_reduce_fusion.9
  475.1 36.1 %shard_map.357 = (f32[2,8,64,256]{3,2,1,0:T(8,128)S(1)}, f32[2,2,2048,64]{3,2,1,0:T(8,128)}, f32[2,2,2048,64]{3,2,1,0:T(8,128)}) custom-call(s32[2,1,256]{2,1,0:T(1,128)S(1)} %broadcast_in_dim.278.low_ref.refs_0_, s32[1,1,256]{2,1,0:T(1,128)S(1)} %iota_add_fusion.1.high_ref.refs_1_, bf16[2,8,256,64]{3,2,1,0:T(8,128)(2,1)S(1)} %copy-done.4, ...), custom_call_target="tpu_custom_call" | custom-call | flops 10737418240 | bytes 25165824 | tf_op jit(solution)/shard_map/pallas_call | solution.py:278
  517.7 4.8 copy.305
  548.3 6.5 multiply_reduce_fusion.6
  554.8 7.7 reduce-scatter.12.cloned.1.call-done
  576.8 40.8 %reduce-scatter.18.cloned.1.call-done = bf16[256,1024]{1,0:T(8,128)(2,1)} async-done(((bf16[2048,1024]{1,0:T(8,128)(2,1)}), bf16[256,1024]{1,0:T(8,128)(2,1)}) %reduce-scatter.18.cloned.1.call-update) | async-done | bytes 524304 | tf_op jit(solution)/shard_map/reduce_scatter | solution.py:330
  617.7 11.1 convolution_convert_fusion
  628.8 8.5 copy.325
  638.6 16.8 %fusion.11 = (f32[2,256,24]{1,2,0:T(8,128)S(1)}, f32[2,256,24]{1,2,0:T(8,128)}, f32[2,256,24]{1,2,0:T(8,128)}, f32[2,256,256]{2,1,0:T(8,128)}) fusion(f32[2,256,24]{1,2,0:T(8,128)S(1)} %copy-done.82, f32[2,256,256]{2,1,0:T(8,128)} %fusion.104, f32[2,256,24]{1,2,0:T(8,128)S(1)} %copy-done.59, pred[2,256,256]{2,1,0:T(8,128)(4,1)S(1)} %copy-done.67, ...), kind=kOutput, calls=%fused_computation.17 | convolution fusion | flops 1254977536 | bytes 7716864 | tf_op jit(solution)/shard_map/transpose(jvp(vmap(ijh,jhp->ihp)))/dot_general | solution.py:107
  655.5 16.6 %reduce-scatter.30.cloned.1.call-done = bf16[256,1024]{1,0:T(8,128)(2,1)} async-done(((bf16[2048,1024]{1,0:T(8,128)(2,1)}), bf16[256,1024]{1,0:T(8,128)(2,1)}) %reduce-scatter.30.cloned.1.call-update) | async-done | bytes 524304 | tf_op jit(solution)/shard_map/reduce_scatter | solution.py:330
  675.0 5.0 reduce-window.24
  680.8 4.2 fusion.90
  686.3 43.5 %reduce-scatter.14.cloned.1.call-done = bf16[128,2304]{1,0:T(8,128)(2,1)} async-done(((bf16[1024,2304]{1,0:T(8,128)(2,1)}), bf16[128,2304]{1,0:T(8,128)(2,1)}) %reduce-scatter.14.cloned.1.call-update) | async-done | bytes 589840 | tf_op jit(solution)/shard_map/reduce_scatter | solution.py:330
  730.4 47.4 %all-gather.38.cloned.1.call-done = bf16[16,24,64,128]{3,2,1,0:T(8,128)(2,1)} async-done(((bf16[2,24,64,128]{3,2,1,0:T(8,128)(2,1)}), bf16[16,24,64,128]{3,2,1,0:T(8,128)(2,1)}) %all-gather.38.cloned.1.call-update) | async-done | bytes 6291472 | tf_op jit(solution)/shard_map/all_gather | solution.py:509
  777.8 4.3 fusion
  788.3 8.2 fusion.48
  800.8 10.9 fusion.141
  822.7 5.0 reduce-window.26
  840.9 33.8 %reduce-scatter.26.cloned.1.call-done = bf16[128,4096]{1,0:T(8,128)(2,1)} async-done(((bf16[1024,4096]{1,0:T(8,128)(2,1)}), bf16[128,4096]{1,0:T(8,128)(2,1)}) %reduce-scatter.26.cloned.1.call-update) | async-done | bytes 1048592 | tf_op jit(solution)/shard_map/reduce_scatter | solution.py:330
  874.7 23.8 %reduce-scatter.32.cloned.1.call-done = bf16[64,1024]{1,0:T(8,128)(2,1)} async-done(((bf16[256,1024]{1,0:T(8,128)(2,1)}), bf16[64,1024]{1,0:T(8,128)(2,1)}) %reduce-scatter.32.cloned.1.call-update) | async-done | bytes 131088 | tf_op jit(solution)/shard_map/reduce_scatter | solution.py:331
  898.6 22.5 %reduce-scatter.16.cloned.1.call-done = bf16[32,2304]{1,0:T(8,128)(2,1)} async-done(((bf16[128,2304]{1,0:T(8,128)(2,1)}), bf16[32,2304]{1,0:T(8,128)(2,1)}) %reduce-scatter.16.cloned.1.call-update) | async-done | bytes 147472 | tf_op jit(solution)/shard_map/reduce_scatter | solution.py:331
  921.2 52.1 %reduce-scatter.22.cloned.1.call-done = bf16[128,1920]{1,0:T(8,128)(2,1)} async-done(((bf16[1024,1920]{1,0:T(8,128)(2,1)}), bf16[128,1920]{1,0:T(8,128)(2,1)}) %reduce-scatter.22.cloned.1.call-update) | async-done | bytes 491536 | tf_op jit(solution)/shard_map/reduce_scatter | solution.py:330
  973.5 6.5 convolution_add_fusion
  980.2 6.9 fusion.24
  987.1 11.5 %all-gather.30.cloned.1.call-done = bf16[512,1024]{1,0:T(8,128)(2,1)} async-done(((bf16[64,1024]{1,0:T(8,128)(2,1)}), bf16[512,1024]{1,0:T(8,128)(2,1)}) %all-gather.30.cloned.1.call-update) | async-done | bytes 1048592 | tf_op jit(solution)/shard_map/all_gather | solution.py:332
  999.6 28.5 %reduce-scatter.28.cloned.1.call-done = bf16[32,4096]{1,0:T(8,128)(2,1)} async-done(((bf16[128,4096]{1,0:T(8,128)(2,1)}), bf16[32,4096]{1,0:T(8,128)(2,1)}) %reduce-scatter.28.cloned.1.call-update) | async-done | bytes 262160 | tf_op jit(solution)/shard_map/reduce_scatter | solution.py:331
  1031.0 21.1 %all-gather.34.cloned.1.call-done = bf16[512,1024]{1,0:T(8,128)(2,1)} async-done(((bf16[64,1024]{1,0:T(8,128)(2,1)}), bf16[512,1024]{1,0:T(8,128)(2,1)}) %all-gather.34.cloned.1.call-update) | async-done | bytes 1048592 | tf_op jit(solution)/shard_map/all_gather | solution.py:332
  1056.6 7.3 fusion.65
  1064.0 40.5 %psum.7 = f32[12616]{0:T(1024)S(1)} all-reduce(f32[12616]{0:T(1024)S(1)} %concatenate.75), channel_id=1, replica_groups=mesh['fsdp'=4,'ctx'=8] {'fsdp','ctx'}, use_global_device_ids=true, to_apply=%region_38.39 | all-reduce | flops 12616 | bytes 100928 | tf_op jit(solution)/shard_map/psum | solution.py:616
  1109.8 4.9 fusion.61
  1120.6 13.4 %all_gather.70 = bf16[256,1920]{1,0:T(8,128)(2,1)S(1)} all-gather(bf16[32,1920]{1,0:T(8,128)(2,1)} %reduce-scatter.24.cloned.1.call-done), channel_id=1, replica_groups=mesh['fsdp'=4,'ctx'=8] {'ctx'}, dimensions={0}, use_global_device_ids=true | all-gather | bytes 1105920 | tf_op jit(solution)/shard_map/all_gather | solution.py:332
  (545 shorter events, 208.2 us)
Async XLA Ops:
  7.2 34.9 %copy-start.24 = (bf16[2,256,1024]{2,1,0:T(8,128)(2,1)S(1)}, bf16[2,256,1024]{2,1,0:T(8,128)(2,1)}, u32[]{:S(2)}) copy-start(bf16[2,256,1024]{2,1,0:T(8,128)(2,1)} %param.23) | copy-start | bytes 3145732
  7.2 85.8 %all-gather.16.cloned.1.call-start = ((), (), s32[]{:S(2)}) async-start(), calls=%async_computation.11 | async-start | bytes 8921088 | tf_op jit(solution)/shard_map/all_gather | solution.py:318
  11.1 154.1 %all-gather.18.cloned.1.call-start = ((), (), s32[]{:S(2)}) async-start(), calls=%async_computation.12 | async-start | bytes 2359296 | tf_op jit(solution)/shard_map/all_gather | solution.py:424
  39.9 66.2 %copy-start.69 = (bf16[4,3154]{1,0:T(4,128)(2,1)}, bf16[4,3154]{1,0:T(4,128)(2,1)S(1)}, u32[]{:S(2)}) copy-start(bf16[4,3154]{1,0:T(4,128)(2,1)S(1)} %reshape.818) | copy-start | bytes 75700
  40.1 52.9 %copy-start.85 = (f32[1,2,4,128]{3,1,2,0:T(2,128)}, f32[1,2,4,128]{3,1,2,0:T(2,128)S(1)}, u32[]{:S(2)}) copy-start(f32[1,2,4,128]{3,1,2,0:T(2,128)S(1)} %copy.355) | copy-start | bytes 12292
  41.7 51.3 %copy-start.104 = (f32[1,2,2,128]{3,1,2,0:T(2,128)}, f32[1,2,2,128]{3,1,2,0:T(2,128)S(1)}, u32[]{:S(2)}) copy-start(f32[1,2,2,128]{3,1,2,0:T(2,128)S(1)} %copy.354) | copy-start | bytes 6148
  41.7 51.3 %copy-start.100 = (f32[512]{0:T(512)}, f32[512]{0:T(512)S(1)}, u32[]{:S(2)}) copy-start(f32[512]{0:T(512)S(1)} %rsqrt.33) | copy-start | bytes 6148
  42.1 62.3 %copy-start.53 = (f32[256,32]{0,1:T(8,128)}, f32[256,32]{0,1:T(8,128)S(1)}, u32[]{:S(2)}) copy-start(f32[256,32]{0,1:T(8,128)S(1)} %get-tuple-element.255) | copy-start | bytes 98308
  42.1 62.3 %copy-start.54 = (f32[256,32]{0,1:T(8,128)}, f32[256,32]{0,1:T(8,128)S(1)}, u32[]{:S(2)}) copy-start(f32[256,32]{0,1:T(8,128)S(1)} %get-tuple-element.254) | copy-start | bytes 98308
  42.4 58.2 %copy-start.43 = (bf16[512,1024]{1,0:T(8,128)(2,1)}, bf16[512,1024]{1,0:T(8,128)(2,1)S(1)}, u32[]{:S(2)}) copy-start(bf16[512,1024]{1,0:T(8,128)(2,1)S(1)} %fusion.64) | copy-start | bytes 3145732
  105.5 94.8 %all-gather.36.cloned.1.call-start = ((), (), s32[]{:S(2)}) async-start(), calls=%async_computation.32 | async-start | bytes 7077888 | tf_op jit(solution)/shard_map/all_gather | solution.py:454
  115.0 7.7 collective-permute-start
  137.7 107.7 %all-gather.22.cloned.1.call-start = ((), (), s32[]{:S(2)}) async-start(), calls=%async_computation.14 | async-start | bytes 3244032 | tf_op jit(solution)/shard_map/all_gather | solution.py:318
  139.3 161.8 %all-gather.20.cloned.1.call-start = ((), (), s32[]{:S(2)}) async-start(), calls=%async_computation.13 | async-start | bytes 1081344 | tf_op jit(solution)/shard_map/all_gather | solution.py:318
  140.8 240.1 %all-gather.24.cloned.1.call-start = ((), (), s32[]{:S(2)}) async-start(), calls=%async_computation.15 | async-start | bytes 8650752 | tf_op jit(solution)/shard_map/all_gather | solution.py:318
  142.6 302.4 %all-gather.26.cloned.1.call-start = ((), (), s32[]{:S(2)}) async-start(), calls=%async_computation.16 | async-start | bytes 4325376 | tf_op jit(solution)/shard_map/all_gather | solution.py:318
  144.3 418.2 %reduce-scatter.12.cloned.1.call-start = ((), (), s32[]{:S(2)}) async-start(), calls=%async_computation.17 | async-start | bytes 2359296 | tf_op jit(solution)/shard_map/reduce_scatter | solution.py:547
  148.2 469.4 %copy-start.87 = (f32[1,2,4,128]{3,1,2,0:T(2,128)}, f32[1,2,4,128]{3,1,2,0:T(2,128)S(1)}, u32[]{:S(2)}) copy-start(f32[1,2,4,128]{3,1,2,0:T(2,128)S(1)} %copy.357) | copy-start | bytes 12292
  245.4 55.8 %copy-start.25 = (bf16[2,256,1024]{2,1,0:T(8,128)(2,1)S(1)}, bf16[2,256,1024]{2,1,0:T(8,128)(2,1)}, u32[]{:S(2)}) copy-start(bf16[2,256,1024]{2,1,0:T(8,128)(2,1)} %param.23) | copy-start | bytes 3145732
  305.4 312.3 %copy-start.102 = (f32[512]{0:T(512)}, f32[512]{0:T(512)S(1)}, u32[]{:S(2)}) copy-start(f32[512]{0:T(512)S(1)} %fusion.128) | copy-start | bytes 6148
  380.9 64.1 %copy-start.32 = (bf16[2,256,1024]{2,1,0:T(8,128)(2,1)S(1)}, bf16[2,256,1024]{2,1,0:T(8,128)(2,1)}, u32[]{:S(2)}) copy-start(bf16[2,256,1024]{2,1,0:T(8,128)(2,1)} %param.24) | copy-start | bytes 3145732
  522.5 95.0 %reduce-scatter.18.cloned.1.call-start = ((), (), s32[]{:S(2)}) async-start(), calls=%async_computation.21 | async-start | bytes 4718592 | tf_op jit(solution)/shard_map/reduce_scatter | solution.py:330
  530.9 141.2 %reduce-scatter.30.cloned.1.call-start = ((), (), s32[]{:S(2)}) async-start(), calls=%async_computation.29 | async-start | bytes 4718592 | tf_op jit(solution)/shard_map/reduce_scatter | solution.py:330
  538.7 191.2 %reduce-scatter.14.cloned.1.call-start = ((), (), s32[]{:S(2)}) async-start(), calls=%async_computation.18 | async-start | bytes 5308416 | tf_op jit(solution)/shard_map/reduce_scatter | solution.py:330
  570.7 207.1 %all-gather.38.cloned.1.call-start = ((), (), s32[]{:S(2)}) async-start(), calls=%async_computation.33 | async-start | bytes 7077888 | tf_op jit(solution)/shard_map/all_gather | solution.py:509
  576.7 263.6 %reduce-scatter.20.cloned.1.call-start = ((), (), s32[]{:S(2)}) async-start(), calls=%async_computation.22 | async-start | bytes 655360 | tf_op jit(solution)/shard_map/reduce_scatter | solution.py:331
  617.6 257.1 %reduce-scatter.26.cloned.1.call-start = ((), (), s32[]{:S(2)}) async-start(), calls=%async_computation.26 | async-start | bytes 9437184 | tf_op jit(solution)/shard_map/reduce_scatter | solution.py:330
  637.3 261.2 %reduce-scatter.32.cloned.1.call-start = ((), (), s32[]{:S(2)}) async-start(), calls=%async_computation.30 | async-start | bytes 655360 | tf_op jit(solution)/shard_map/reduce_scatter | solution.py:331
  672.2 249.0 %reduce-scatter.16.cloned.1.call-start = ((), (), s32[]{:S(2)}) async-start(), calls=%async_computation.19 | async-start | bytes 737280 | tf_op jit(solution)/shard_map/reduce_scatter | solution.py:331
  680.8 97.0 %copy-start.95 = (f32[8,2,24]{2,1,0:T(2,128)S(1)}, f32[8,2,24]{2,1,0:T(2,128)}, u32[]{:S(2)}) copy-start(f32[8,2,24]{2,1,0:T(2,128)} %broadcast_select_fusion) | copy-start | bytes 4612
  729.9 243.4 %reduce-scatter.22.cloned.1.call-start = ((), (), s32[]{:S(2)}) async-start(), calls=%async_computation.24 | async-start | bytes 4423680 | tf_op jit(solution)/shard_map/reduce_scatter | solution.py:330
  820.6 9.3 collective-permute-start.1
  840.2 133.2 %copy-start.23 = (f32[512,1024]{1,0:T(8,128)S(1)}, f32[512,1024]{1,0:T(8,128)}, u32[]{:S(2)}) copy-start(f32[512,1024]{1,0:T(8,128)} %get-tuple-element.257) | copy-start | bytes 6291460
  840.2 158.4 %all-gather.30.cloned.1.call-start = ((), (), s32[]{:S(2)}) async-start(), calls=%async_computation.23 | async-start | bytes 1179648 | tf_op jit(solution)/shard_map/all_gather | solution.py:332
  840.8 187.2 %reduce-scatter.28.cloned.1.call-start = ((), (), s32[]{:S(2)}) async-start(), calls=%async_computation.27 | async-start | bytes 1310720 | tf_op jit(solution)/shard_map/reduce_scatter | solution.py:331
  874.7 177.4 %all-gather.34.cloned.1.call-start = ((), (), s32[]{:S(2)}) async-start(), calls=%async_computation.31 | async-start | bytes 1179648 | tf_op jit(solution)/shard_map/all_gather | solution.py:332
  898.6 216.1 %all-gather.28.cloned.1.call-start = ((), (), s32[]{:S(2)}) async-start(), calls=%async_computation.20 | async-start | bytes 1327104 | tf_op jit(solution)/shard_map/all_gather | solution.py:332
  921.2 199.4 %reduce-scatter.24.cloned.1.call-start = ((), (), s32[]{:S(2)}) async-start(), calls=%async_computation.25 | async-start | bytes 614400 | tf_op jit(solution)/shard_map/reduce_scatter | solution.py:331
  973.4 164.9 %all-gather.32.cloned.1.call-start = ((), (), s32[]{:S(2)}) async-start(), calls=%async_computation.28 | async-start | bytes 2359296 | tf_op jit(solution)/shard_map/all_gather | solution.py:332
  1031.0 25.4 %copy-start.90 = (f32[1792]{0:T(1024)S(1)}, f32[1792]{0:T(1024)}, u32[]{:S(2)}) copy-start(f32[1792]{0:T(1024)} %get-tuple-element.175) | copy-start | bytes 21508
  1031.0 25.4 %copy-start.89 = (f32[1792]{0:T(1024)S(1)}, f32[1792]{0:T(1024)}, u32[]{:S(2)}) copy-start(f32[1792]{0:T(1024)} %get-tuple-element.177) | copy-start | bytes 21508
  1031.0 25.5 %copy-start.26 = (bf16[2,256,1024]{2,1,0:T(8,128)(2,1)S(1)}, bf16[2,256,1024]{2,1,0:T(8,128)(2,1)}, u32[]{:S(2)}) copy-start(bf16[2,256,1024]{2,1,0:T(8,128)(2,1)} %param.23) | copy-start | bytes 3145732
  1031.0 25.5 %copy-start.86 = (f32[1,2,4,128]{3,1,2,0:T(2,128)S(1)}, f32[1,2,4,128]{3,1,2,0:T(2,128)}, u32[]{:S(2)}) copy-start(f32[1,2,4,128]{3,1,2,0:T(2,128)} %copy-done.85) | copy-start | bytes 12292
  1031.0 25.5 %copy-start.101 = (f32[512]{0:T(512)S(1)}, f32[512]{0:T(512)}, u32[]{:S(2)}) copy-start(f32[512]{0:T(512)} %copy-done.100) | copy-start | bytes 6148
  1056.6 53.2 %copy-start.105 = (f32[1,2,2,128]{3,1,2,0:T(2,128)S(1)}, f32[1,2,2,128]{3,1,2,0:T(2,128)}, u32[]{:S(2)}) copy-start(f32[1,2,2,128]{3,1,2,0:T(2,128)} %copy-done.104) | copy-start | bytes 6148
  1056.6 53.2 %copy-start.88 = (f32[1,2,4,128]{3,1,2,0:T(2,128)S(1)}, f32[1,2,4,128]{3,1,2,0:T(2,128)}, u32[]{:S(2)}) copy-start(f32[1,2,4,128]{3,1,2,0:T(2,128)} %copy-done.87) | copy-start | bytes 12292
  1056.6 53.2 %copy-start.99 = (f32[512]{0:T(512)S(1)}, f32[512]{0:T(512)}, u32[]{:S(2)}) copy-start(f32[512]{0:T(512)} %copy-done.98) | copy-start | bytes 6148
  1056.6 53.2 %copy-start.103 = (f32[512]{0:T(512)S(1)}, f32[512]{0:T(512)}, u32[]{:S(2)}) copy-start(f32[512]{0:T(512)} %copy-done.102) | copy-start | bytes 6148
  (118 other events, 788.7 us)
Sparse Core Ops, SparseCore 0:
  11.5 81.4 all-gather.15
  105.6 26.7 all-gather.17
  137.8 45.1 all-gather.35
  186.3 59.0 all-gather.21
  248.6 52.4 all-gather.19
  304.4 76.4 all-gather.23
  384.3 60.6 all-gather.25
  522.7 39.7 reduce-scatter.11
  566.2 51.3 reduce-scatter.17
  620.8 51.2 reduce-scatter.29
  676.0 53.8 reduce-scatter.13
  732.2 45.5 all-gather.37
  780.0 21.6 reduce-scatter.19
  805.0 69.5 reduce-scatter.25
  876.9 21.6 reduce-scatter.31
  900.8 20.3 reduce-scatter.15
  924.9 48.3 reduce-scatter.21
  975.1 23.4 all-gather.29
  1000.9 27.1 reduce-scatter.27
  1029.9 22.1 all-gather.33
  1054.2 24.0 all-gather.27
  1080.7 21.5 reduce-scatter.23
  1104.1 27.5 all-gather.31
